TPU v7x, 32 devices: a whole 2x2x4 slice. The times are simulated.
32 devices in a mesh: dp: 4 (over x, core), seq: 8 (over z, y).
Axes of the slice: x: 2, y: 2, z: 4, core: 2. Of those that a mesh axis runs over, the one named last changes fastest.
Arguments:
- tokens: bfloat16 [6144, 2048], P(('dp', 'seq')), may hold values from -6 to 6
- lengths: int32 [4, 8], P('dp'), may hold values from 0 to 1536, as said below
- cotangent: bfloat16 [6144, 2048], P(('dp', 'seq')), may hold values from -6 to 6
- norm_one: bfloat16 [2048], P(('dp', 'seq')), may hold values from 0.5 to 1.5
- query_down: bfloat16 [2048, 1024], P(('dp', 'seq')), may hold values from -0.125 to 0.125
- query_gain: bfloat16 [1024], P(('dp', 'seq')), may hold values from 0.5 to 1.5
- query_up: bfloat16 [1024, 4096], P(('dp', 'seq')), may hold values from -0.1875 to 0.1875
- key_proj: bfloat16 [2048, 256], P(('dp', 'seq')), may hold values from -0.125 to 0.125
- value_proj: bfloat16 [2048, 256], P(('dp', 'seq')), may hold values from -0.125 to 0.125
- out_proj: bfloat16 [4096, 2048], P(('dp', 'seq')), may hold values from -0.75 to 0.75
- norm_two: bfloat16 [2048], P(('dp', 'seq')), may hold values from 0.5 to 1.5
- gate_proj: bfloat16 [2048, 5632], P(('dp', 'seq')), may hold values from -0.125 to 0.125
- up_proj: bfloat16 [2048, 5632], P(('dp', 'seq')), may hold values from -0.125 to 0.125
- down_proj: bfloat16 [5632, 2048], P(('dp', 'seq')), may hold values from -0.078125 to 0.078125
Outputs:
- output: bfloat16 [6144, 2048], P(('dp', 'seq'))
- grad_tokens: float32 [6144, 2048], P(('dp', 'seq'))
- grad_norm_one: float32 [2048], P(('dp', 'seq'))
- grad_query_down: float32 [2048, 1024], P(('dp', 'seq'))
- grad_query_gain: float32 [1024], P(('dp', 'seq'))
- grad_query_up: float32 [1024, 4096], P(('dp', 'seq'))
- grad_key_proj: float32 [2048, 256], P(('dp', 'seq'))
- grad_value_proj: float32 [2048, 256], P(('dp', 'seq'))
- grad_out_proj: float32 [4096, 2048], P(('dp', 'seq'))
- grad_norm_two: float32 [2048], P(('dp', 'seq'))
- grad_gate_proj: float32 [2048, 5632], P(('dp', 'seq'))
- grad_up_proj: float32 [2048, 5632], P(('dp', 'seq'))
- grad_down_proj: float32 [5632, 2048], P(('dp', 'seq'))
Inputs may be any that keep to these rules, and one draw needn't show every extreme that they name: In one row, drawn from the seed, a single document fills all 1536 slots and the other entries are 0; every other row is filled to between 7/10 and 9/10 of its slots, the rest being padding, with documents of uneven lengths.
All inputs are finite; a program needn't handle non-finite values.
Results may differ from a plain program's by a relative error of at most 0.017.
Values may be sent and summed in bfloat16 or wider, within the bound.
A program may use at most 512 MiB of HBM per device.

v0:
```python
import functools
import math

import jax
import jax.numpy as jnp
from jax import lax
from jax.experimental import pallas as pl
from jax.experimental.pallas import tpu as pltpu
from jax.sharding import Mesh, PartitionSpec as P

norm_eps = 1e-05
masked_value = -1e30
every = ("x", "c", "h", "l", "y")
group = ("c", "l", "y")
low = jnp.bfloat16
wide = jnp.float32


def rms_scale(values):
    return lax.rsqrt(jnp.mean(values * values, axis=-1, keepdims=True) + norm_eps)


def rotate(values, cosine, sine):
    half = values.shape[-1] // 2
    a, b = values[..., :half], values[..., half:]
    return jnp.concatenate([a * cosine - b * sine, b * cosine + a * sine], axis=-1)


def rotate_back(values, cosine, sine):
    half = values.shape[-1] // 2
    a, b = values[..., :half], values[..., half:]
    return jnp.concatenate([a * cosine + b * sine, b * cosine - a * sine], axis=-1)


def norm_back(incoming, source, scale, gain):
    weighted = incoming * gain
    source_grad = scale * weighted - source * (scale * scale * scale) * jnp.mean(
        weighted * source, axis=-1, keepdims=True
    )
    return source_grad, jnp.sum(incoming * source * scale, axis=0)


def dot(left, right, out=wide):
    return jnp.dot(left, right, preferred_element_type=wide).astype(out)


def outer_sum(left, right, out=wide):
    return lax.dot_general(
        left, right, (((0,), (0,)), ((), ())), preferred_element_type=wide
    ).astype(out)


def times_transposed(left, right, out=wide):
    return lax.dot_general(
        left, right, (((1,), (1,)), ((), ())), preferred_element_type=wide
    ).astype(out)


def pick(array, index, axis=0):
    return lax.dynamic_index_in_dim(array, index, axis, keepdims=False)


def after(value, *done):
    return lax.optimization_barrier((value,) + done)[0]


def together(*values):
    return lax.optimization_barrier(values)


def flip(value, axis):
    return lax.ppermute(value, axis, [(0, 1), (1, 0)])


def flip_cross(value):
    return lax.ppermute(value, ("c", "h"), [(1, 2), (2, 1)])


def choose_home(value, moved):
    return jnp.where(lax.axis_index("c") == lax.axis_index("h"), value, moved)


def swap_home(value):
    return choose_home(value, flip_cross(value))


def group_place():
    return (
        lax.axis_index("c") * lax.axis_size("l") + lax.axis_index("l")
    ) * 2 + lax.axis_index("y")


def all_to_all_row(blocks):
    return lax.all_to_all(blocks, group, 0, 0, tiled=True)


def send(value, offsets):
    return lax.ppermute(value, group, [(i, i ^ offsets[i // 4]) for i in range(8)])


def scatter_row_async(state, stage):
    core = lax.axis_index("c")
    me = lax.axis_index("l") * 2 + lax.axis_index("y")
    first, second = 1 + core, 2 - core
    if stage == 0:
        return state[0], flip(state[1], "c")
    own, moved = state[:2]

    def block(index):
        return pick(own, index).astype(wide) + pick(moved, index).astype(wide)

    if stage == 1:
        far = send(block(me ^ 3).astype(low), (2, 1))
        return own, moved, far, send(block(me ^ second).astype(low), (2, 1))
    far, side = state[2:4]
    if stage == 2:
        return state + (send((block(me ^ first) + far.astype(wide)).astype(low), (1, 2)),)
    return block(me) + side.astype(wide) + state[4].astype(wide)


def sum_columns(terms, h_dim):
    for axis, dim in (("x", 0), ("h", h_dim)):
        terms = jnp.moveaxis(terms, dim, 0).astype(wide)
        terms = lax.psum_scatter(terms, axis, scatter_dimension=0, tiled=False).astype(low)
    return terms


def halves(terms, axis, dim):
    me = lax.axis_index(axis)
    return pick(terms, me, dim), flip(pick(terms, 1 - me, dim), axis)


def add(own, came):
    return (own.astype(wide) + came.astype(wide)).astype(low)


def other(value, flag=1):
    return value + flag * (1 - 2 * value)


def greet(peers):
    barrier = pltpu.get_barrier_semaphore()
    for peer in peers:
        pl.semaphore_signal(barrier, inc=1, device_id=peer, device_id_type=pl.DeviceIdType.MESH)
    pl.semaphore_wait(barrier, len(peers))


def remote(source, target, send_sem, recv_sem, peer):
    return pltpu.make_async_remote_copy(
        src_ref=source,
        dst_ref=target,
        send_sem=send_sem,
        recv_sem=recv_sem,
        device_id=peer,
        device_id_type=pl.DeviceIdType.MESH,
    )


def in_hbm():
    return pl.BlockSpec(memory_space=pl.ANY)


def open_kernel(n_swaps, part, order, small_ref, out_ref, heads_in, gate_in, up_in, *refs):
    n_sets = 3
    swaps, refs = refs[:n_swaps], refs[n_swaps:]
    (full_ref, heads_ref), refs = refs[:2], refs[2:]
    set_outs, refs = refs[:n_sets], refs[n_sets:]
    swap_outs, refs = refs[:n_swaps], refs[n_swaps:]
    (small_buf, out_buf), refs = refs[:2], refs[2:]
    raws, set_bufs, refs = refs[:2], refs[2:5], refs[5:]
    heads_buf, splits = set_bufs[0], set_bufs[1:]
    sets = [heads_in, *splits]
    swap_bufs, refs = refs[:n_swaps], refs[n_swaps:]
    sends, recvs, swap_sends, swap_recvs, set_sends, set_recvs, out_sems, head_sems, loads_sem, stores_sem, split_sem = refs
    x, c, h, l, y = [lax.axis_index(a) for a in every]
    hops = {
        1: {"h": other(h)},
        2: {"l": other(l)},
        4: {"y": other(y)},
        8: {"x": other(x)},
        16: {"c": other(c)},
    }
    cross = {"c": other(c), "h": other(h)}
    me = (c * 2 + l) * 2 + y

    def group_peer(k):
        return {"c": other(c, k // 4), "l": other(l, k // 2 % 2), "y": other(y, k % 2)}

    def group_index(k):
        peer = group_peer(k)
        return (peer["c"] * 2 + peer["l"]) * 2 + peer["y"]

    def index(code):
        at_x, at_l = other(x, code // 8 % 2), other(l, code // 2 % 2)
        return (((at_x * 2 + c) * 2 + other(h, code % 2)) * 2 + at_l) * 2 + other(y, code // 4 % 2)

    beside, corner = {"y": other(y)}, {"h": other(h), "y": h}
    greet(
        [hops[1], hops[8], cross, {"h": other(h), "y": other(y)}]
        + [group_peer(k) for k in range(1, 8)]
    )
    copies = []
    half = heads_ref.at[y]
    to_beside = remote(out_ref, half, out_sems.at[0], out_sems.at[1], beside)
    differ = y + h - 2 * y * h
    to_corner = remote(out_ref, half, out_sems.at[2], out_sems.at[3 + differ], corner)

    def push(code):
        block = full_ref.at[index(code)]
        source = small_ref if code == 0 else block
        for hop in (1, 2, 4, 8, 16):
            if code < hop:
                name = code + hop
                copy = remote(source, block, sends.at[name], recvs.at[name], hops[hop])
                copy.start()
                copies.append(copy)

    def set_slot(i):
        return set_outs[0].at[x, c, h, l * 2 + y] if i == 0 else set_outs[i].at[me]

    set_copies = []

    def set_push(i):
        for k in range(1, 8):
            copy = remote(
                sets[i].at[group_index(k)], set_slot(i), set_sends.at[i, k], set_recvs.at[i, k],
                group_peer(k),
            )
            copy.start()
            set_copies.append(copy)

    push(0)
    set_push(0)
    moving = [
        remote(source, target, swap_sends.at[i], swap_recvs.at[i], cross)
        for i, (source, target) in enumerate(zip(swaps, swap_outs))
    ]

    def push_moves():
        @pl.when(c != h)
        def _():
            for copy in moving:
                copy.start()

        @pl.when(y != h)
        def _():
            to_beside.start()

        to_corner.start()

    loads, stores = [], []
    raw_loads = [
        pltpu.make_async_copy(source, raw, stores_sem.at[3 + n_swaps + i])
        for i, (source, raw) in enumerate(((gate_in, raws[0]), (up_in, raws[1])))
    ]
    for load in raw_loads:
        load.start()
    locals_in = [small_ref, out_ref, heads_in.at[me]] + list(swaps)
    locals_buf = [small_buf, out_buf, heads_buf] + list(swap_bufs)
    locals_out = [full_ref.at[index(0)], half, set_slot(0)]
    for i, (source, buf) in enumerate(zip(locals_in, locals_buf)):
        loads.append(pltpu.make_async_copy(source, buf, loads_sem.at[i]))
        loads[-1].start()
    for load in loads:
        load.wait()
    for i, (buf, target) in enumerate(zip(locals_buf, locals_out)):
        stores.append(pltpu.make_async_copy(buf, target, stores_sem.at[i]))
    keep_out = stores.pop(1)
    for store in stores:
        store.start()

    @pl.when(y == h)
    def _():
        keep_out.start()

    keeps = [
        pltpu.make_async_copy(buf, target, stores_sem.at[3 + i])
        for i, (buf, target) in enumerate(zip(swap_bufs, swap_outs))
    ]

    @pl.when(c == h)
    def _():
        for keep in keeps:
            keep.start()

    def arrived(name):
        remote(small_ref, small_ref, sends.at[name], recvs.at[name], hops[16]).wait_recv()

    def head_copy(at_h, slot, peer):
        part = set_outs[0].at[x, :, at_h]
        copy = remote(part, part, head_sems.at[slot], head_sems.at[3 + slot], peer)
        copy.start()
        return copy

    head_copies, split_keeps = [], []
    for n, code in enumerate((2, 4, 1, 6, 3, 5, 7, 8, 9, 10, 11, 12, 13, 14, 15)):
        arrived(code)
        push(code)
        if n == 2:
            for copy in set_copies:
                copy.wait()
            for store in stores:
                store.wait()
            done = len(set_copies)
            for load in raw_loads:
                load.wait()
            split_kernel(part, order, *raws, *splits)
            for i in range(1, n_sets):
                set_push(i)
                keep = pltpu.make_async_copy(splits[i - 1].at[me], set_slot(i), split_sem.at[i - 1])
                keep.start()
                split_keeps.append(keep)
            head_copies.append(head_copy(h, 0, hops[1]))
            head_copies.append(head_copy(h, 1, hops[8]))
            push_moves()
        if n == 9:
            head_copies[0].wait_recv()
            head_copies.append(head_copy(other(h), 2, hops[8]))
    for code in range(16):
        arrived(16 + code)
    for copy in copies:
        copy.wait_send()
    for copy in set_copies[done:] + split_keeps:
        copy.wait()
    head_copies[0].wait_send()
    for copy in head_copies[1:]:
        copy.wait()
    to_corner.wait_send()

    @pl.when(y != h)
    def _():
        to_beside.wait_send()
        remote(out_ref, half, out_sems.at[2], out_sems.at[3], corner).wait_recv()
        remote(out_ref, half, out_sems.at[2], out_sems.at[4], corner).wait_recv()

    @pl.when(y == h)
    def _():
        keep_out.wait()
        to_beside.wait_recv()

    @pl.when(c != h)
    def _():
        for copy in moving:
            copy.wait()

    @pl.when(c == h)
    def _():
        for keep in keeps:
            keep.wait()


def open_exchange(small, out_rows, heads, gate, up, swaps, part, order, total):
    n_swaps = len(swaps)
    args = [small, out_rows, heads, gate, up] + swaps
    split = (len(order), gate.shape[0], total)
    shapes = [(32,) + small.shape, (2,) + out_rows.shape, (2, 2, 2, 4) + heads.shape[1:], split, split]
    out_shape = [jax.ShapeDtypeStruct(s, low) for s in shapes]
    out_shape += [jax.ShapeDtypeStruct(a.shape, a.dtype) for a in swaps]
    sem = pltpu.SemaphoreType.DMA
    out = pl.pallas_call(
        functools.partial(open_kernel, n_swaps, part, order),
        in_specs=[in_hbm()] * len(args),
        out_specs=[in_hbm()] * len(out_shape),
        out_shape=out_shape,
        scratch_shapes=[pltpu.VMEM(a.shape, low) for a in (small, out_rows, gate, up)]
        + [pltpu.VMEM(s, low) for s in (heads.shape[1:], split, split)]
        + [pltpu.VMEM(a.shape, a.dtype) for a in swaps]
        + [sem((32,)), sem((32,)), sem((n_swaps,)), sem((n_swaps,))]
        + [sem((3, 8)), sem((3, 8)), sem((5,)), sem((6,))]
        + [sem((3 + n_swaps,)), sem((5 + n_swaps,)), sem((2,))],
        compiler_params=pltpu.CompilerParams(
            collective_id=1, has_side_effects=True, vmem_limit_bytes=16 * 1024 * 1024
        ),
        cost_estimate=pl.CostEstimate(flops=0, bytes_accessed=150 * 1024 * 1024, transcendentals=0),
        name="open_exchange",
    )(*args)
    return out[0], out[1], out[2:5], out[5:]


def row_peers(even):
    c, l, y = [lax.axis_index(a) for a in group]
    if even == "l":
        near = {"l": l, "y": other(y)}
        side = {"l": other(l), "y": y}
    elif even:
        near = {"l": other(l, c), "y": other(y, 1 - c)}
        side = {"l": other(l, 1 - c), "y": other(y, c)}
    else:
        near = {"l": other(l), "y": y}
        side = {"l": l, "y": other(y)}
    return c, l, y, near, side, {"c": other(c)}


def turn(values, cosine, sine):
    half = values.shape[1] // 2
    a, b = values[:, :half], values[:, half:]
    return a * cosine - b * sine, b * cosine + a * sine


def angles(ends_ref, rates, begin, count):
    places = begin + lax.broadcasted_iota(jnp.int32, (count, 1), 0)
    start = jnp.zeros_like(places)
    for j in range(ends_ref.shape[0]):
        end = ends_ref[j]
        start = jnp.where(places >= end, end, start)
    phases = (places - start).astype(wide) * rates
    return jnp.cos(phases), jnp.sin(phases)


def front_kernel(kinds, ends_ref, home_ref, full_ref, gain_ref, low_gain_ref, rates_ref, *refs):
    n = len(kinds)
    more, refs = refs[:n], refs[n:]
    out_ref, hidden_ref, latent_ref, cos_ref, sin_ref, refs = *refs[:5], refs[5:]
    more_out, refs = refs[:n], refs[n:]
    full, own, sends, recvs, load_sem, store_sem, more_sems = refs
    beside = Beside(kinds, more, more_out, more_sems)
    flow = RowGather(False, sends.shape[1], own, out_ref, sends, recvs)
    load = pltpu.make_async_copy(full_ref, full, load_sem)
    load.start()
    near, side, twin = flow.peers
    greet([near, side, twin, *beside.peers])
    count = home_ref.shape[0]
    low_width, head_dim = latent_ref.shape[1], 2 * cos_ref.shape[1]
    half = head_dim // 2
    values = home_ref[...].astype(wide)
    hidden = (values * rms_scale(values) * gain_ref[...]).astype(low)
    hidden_ref[...] = hidden
    cosine, sine = angles(ends_ref, rates_ref[...], flow.me * count, count)
    load.wait()
    mapped = jnp.dot(hidden, full[...], preferred_element_type=wide)
    latent = mapped[:, :low_width]
    latent_ref[...] = latent
    own[:, :low_width] = (latent * rms_scale(latent) * low_gain_ref[...]).astype(low)
    a, b = turn(mapped[:, low_width : low_width + head_dim], cosine, sine)
    own[:, low_width : low_width + half] = a.astype(low)
    own[:, low_width + half : low_width + head_dim] = b.astype(low)
    end = low_width + 2 * head_dim
    own[:, low_width + head_dim :] = mapped[:, low_width + head_dim : end].astype(low)
    flow.begin(None)
    beside.start()
    store = pltpu.make_async_copy(own, out_ref.at[flow.me], store_sem)
    store.start()

    def tables(begin, rows):
        cos_ref[begin : begin + rows, :], sin_ref[begin : begin + rows, :] = angles(
            ends_ref, rates_ref[...], begin, rows
        )

    quarter = cos_ref.shape[0] // 4
    tables(0, quarter)
    tables(quarter, quarter)
    flow.take_near()
    tables(2 * quarter, quarter)
    flow.take_side()
    tables(3 * quarter, quarter)
    flow.take_far()
    for slot in (3, 4, 5, 6):
        flow.take(slot)
    flow.end()
    store.wait()
    beside.wait()


def front(ends, home, in_full, gain_one, gain_latent, rates, row_len, number, kinds, more):
    count, width = home.shape
    low_width = gain_latent.shape[1]
    half = rates.shape[1]
    packed = (count, low_width + 4 * half)
    vmem, sem = pl.BlockSpec(memory_space=pltpu.VMEM), pltpu.SemaphoreType.DMA
    out = pl.pallas_call(
        functools.partial(front_kernel, kinds),
        in_specs=[pl.BlockSpec(memory_space=pltpu.SMEM), vmem, in_hbm(), vmem, vmem, vmem]
        + [in_hbm()] * len(more),
        out_specs=[in_hbm()] + [vmem] * 4 + [in_hbm()] * len(more),
        out_shape=[
            jax.ShapeDtypeStruct((8,) + packed, low),
            jax.ShapeDtypeStruct((count, width), low),
            jax.ShapeDtypeStruct((count, low_width), wide),
            jax.ShapeDtypeStruct((row_len, half), wide),
            jax.ShapeDtypeStruct((row_len, half), wide),
        ]
        + [jax.ShapeDtypeStruct(a.shape, low) for a in more],
        scratch_shapes=[
            pltpu.VMEM(in_full.shape, low),
            pltpu.VMEM(packed, low),
            sem((7, 4)),
            sem((7, 4)),
            sem,
            sem,
            sem((2, len(more))),
        ],
        compiler_params=pltpu.CompilerParams(
            collective_id=number, has_side_effects=True, vmem_limit_bytes=32 * 1024 * 1024
        ),
        cost_estimate=pl.CostEstimate(flops=0, bytes_accessed=100 * 1024 * 1024, transcendentals=0),
        name="front",
    )(ends, home, in_full, gain_one, gain_latent, rates, *more)
    return (out[0].reshape(-1, packed[1]), *out[1:])


def gather_kernel(even, chunks, kinds, own_ref, *refs):
    n = len(kinds)
    more, out_ref, more_out = refs[:n], refs[n], refs[n + 1 : 2 * n + 1]
    buf, sends, recvs, local_sems = refs[2 * n + 1 : 2 * n + 5]
    beside = Beside(kinds, more, more_out, refs[-1])
    flow = RowGather(even, chunks, own_ref, out_ref, sends, recvs)
    flow.begin(beside.peers)
    beside.start()
    load = pltpu.make_async_copy(own_ref, buf, local_sems.at[0])
    load.start()
    load.wait()
    store = pltpu.make_async_copy(buf, out_ref.at[flow.me], local_sems.at[1])
    store.start()
    flow.take_near()
    flow.take_side()
    flow.take_far()
    for slot in (3, 4, 5, 6):
        flow.take(slot)
    flow.end()
    store.wait()
    beside.wait()


class Beside:
    def __init__(self, kinds, sources, targets, sems):
        x, c, h = [lax.axis_index(a) for a in ("x", "c", "h")]
        ways = {"x": {"x": other(x)}, "h": {"h": other(h)}, "cross": {"c": other(c), "h": other(h)}}
        self.peers = [ways[k] for k in sorted(set(kinds))]
        self.moves = c != h
        self.copies = [
            (kind, remote(source, target, sems.at[0, i], sems.at[1, i], ways[kind]))
            for i, (kind, source, target) in enumerate(zip(kinds, sources, targets))
        ]

    def start(self, span=slice(None)):
        for kind, copy in self.copies[span]:
            if kind == "cross":
                pl.when(self.moves)(copy.start)
            else:
                copy.start()

    def wait(self, span=slice(None)):
        for kind, copy in self.copies[span]:
            if kind == "cross":
                pl.when(self.moves)(copy.wait)
            else:
                copy.wait()


class RowGather:
    def __init__(self, even, chunks, own_ref, out_ref, sends, recvs, in_slots=False):
        c, l, y, near, side, twin = row_peers(even)
        self.peers = near, side, twin
        self.chunks, self.rows = chunks, own_ref.shape[0] // chunks
        self.own_ref, self.out_ref, self.sends, self.recvs = own_ref, out_ref, sends, recvs
        at = l * 2 + y
        near_at, side_at = near["l"] * 2 + near["y"], side["l"] * 2 + side["y"]
        far_at = other(l) * 2 + other(y)
        self.me = c * 4 + at
        self.places = [c * 4 + p for p in (near_at, side_at, far_at)]
        swapped = even is True
        twins = (at, side_at, near_at, far_at) if swapped else (at, near_at, side_at, far_at)
        self.places += [other(c) * 4 + p for p in twins]
        self.copies = []
        self.lands = (2, 3, 6, 1, 4, 5, 7) if in_slots else None

    def land(self, slot):
        return self.lands[slot] if self.lands else self.places[slot]

    def start(self, held, k, slot, peer):
        span = pl.ds(k * self.rows, self.rows)
        source = self.own_ref.at[span] if held is None else self.out_ref.at[self.land(held), span]
        if self.lands:
            target = self.out_ref.at[self.lands[slot], span]
        else:
            target = self.out_ref.at[self.me if held is None else self.places[held], span]
        copy = remote(source, target, self.sends.at[slot, k], self.recvs.at[slot, k], peer)
        copy.start()
        self.copies.append(copy)

    def begin(self, more_peers=()):
        near, side, twin = self.peers
        if more_peers is not None:
            greet([near, side, twin, *more_peers])
        for k in range(self.chunks):
            self.start(None, k, 0, near)
            self.start(None, k, 1, side)
            self.start(None, k, 3, twin)

    def arrived(self, slot, k):
        span = self.own_ref.at[pl.ds(k * self.rows, self.rows)]
        target = self.out_ref.at[self.land(slot), pl.ds(k * self.rows, self.rows)]
        remote(
            span, target, self.sends.at[slot, k], self.recvs.at[slot, k], self.peers[2]
        ).wait_recv()

    def take(self, slot):
        for k in range(self.chunks):
            self.arrived(slot, k)

    def take_near(self):
        near, side, twin = self.peers
        for k in range(self.chunks):
            self.arrived(0, k)
            self.start(0, k, 2, side)
            self.start(0, k, 4, twin)

    def take_side(self):
        for k in range(self.chunks):
            self.arrived(1, k)
            self.start(1, k, 5, self.peers[2])

    def take_far(self):
        for k in range(self.chunks):
            self.arrived(2, k)
            self.start(2, k, 6, self.peers[2])

    def end(self):
        for copy in self.copies:
            copy.wait_send()


def gather_row(value, number, even=False, kinds=(), more=()):
    if lax.axis_size("l") != 2:
        return lax.all_gather(value, group, axis=0, tiled=True)
    chunks = 4 if value.shape[0] % 64 == 0 else 1
    args = [value, *more]
    out_shape = [jax.ShapeDtypeStruct((8,) + value.shape, low)]
    out_shape += [jax.ShapeDtypeStruct(a.shape, low) for a in more]
    out = pl.pallas_call(
        functools.partial(gather_kernel, even, chunks, kinds),
        in_specs=[in_hbm()] * len(args),
        out_specs=[in_hbm()] * len(args),
        out_shape=out_shape,
        scratch_shapes=[
            pltpu.VMEM(value.shape, low),
            pltpu.SemaphoreType.DMA((7, chunks)),
            pltpu.SemaphoreType.DMA((7, chunks)),
            pltpu.SemaphoreType.DMA((2,)),
            pltpu.SemaphoreType.DMA((2, max(1, len(more)))),
        ],
        compiler_params=pltpu.CompilerParams(
            collective_id=number, has_side_effects=True, vmem_limit_bytes=16 * 1024 * 1024
        ),
        cost_estimate=pl.CostEstimate(flops=0, bytes_accessed=80 * 1024 * 1024, transcendentals=0),
        name="gather_row",
    )(*args)
    rows = out[0].reshape(-1, value.shape[1])
    return (rows, *out[1:]) if kinds else rows


def load_columns(pieces, target, sem, first):
    x, h = lax.axis_index("x"), lax.axis_index("h")
    rows = pieces[0].shape[0]
    loads = []
    for i, piece in enumerate(pieces):
        at_x = x if i < 4 else other(x)
        at_h = h if i // 2 % 2 == 0 else other(h)
        at = pl.multiple_of(((at_x * 2 + i % 2) * 2 + at_h) * rows, rows)
        loads.append(
            pltpu.make_async_copy(piece, target.at[pl.ds(at, rows)], sem.at[first + i])
        )
    return loads


def load_rows(parts, target, sem):
    x, h = lax.axis_index("x"), lax.axis_index("h")
    rows, width = parts[0][0].shape
    loads = []
    for s, part in enumerate(parts):
        for i, (at_x, at_h) in enumerate(
            ((x, h), (x, other(h)), (other(x), h), (other(x), other(h)))
        ):
            at = pl.multiple_of((at_x * 2 + at_h) * rows, 16)
            loads.append(
                pltpu.make_async_copy(
                    part[i],
                    target.at[pl.ds(at, rows), pl.ds(s * width, width)],
                    sem.at[len(loads)],
                )
            )
            loads[-1].start()
    return loads


def wait_all(copies):
    for copy in copies:
        copy.wait()


def for_tiles(total, tile, body):
    def step(j, carry):
        body(pl.ds(pl.multiple_of(j * tile, tile), tile))
        return carry

    lax.fori_loop(0, total // tile, step, 0)


def feed_kernel(even, chunks, *refs):
    own_ref, gates, ups = refs[0], refs[1:9], refs[9:17]
    downs, grad_ref, refs = refs[17:21], refs[21], refs[22:]
    all_ref, inner_ref, a_ref, b_ref = refs[:4]
    downs_x, home_ref, grads_ref, refs = refs[4:8], refs[8], refs[9], refs[10:]
    xs, wg, wu, inner_s, a_s, b_s, grad_buf, sends, recvs, grad_sends, grad_recvs = refs[:11]
    weight_sems, store_sems, own_sem, more_sems, grad_sems = refs[11:]
    flow = RowGather(even, chunks, own_ref, xs, sends, recvs, in_slots=True)
    beside = Beside(
        ("cross", "x", "x", "x", "x"),
        (grad_ref, *downs),
        (home_ref, *downs_x),
        more_sems,
    )
    away = lax.axis_index("c") != lax.axis_index("h")
    grad_flow = RowGather(True, chunks, home_ref, grads_ref, grad_sends, grad_recvs)
    flow.begin(beside.peers)
    beside.start()
    grad_load = pltpu.make_async_copy(grad_ref, grad_buf, grad_sems.at[0])
    grad_load.start()
    own_load = pltpu.make_async_copy(own_ref, xs.at[0], own_sem)
    own_load.start()
    weights = load_columns(gates, wg, weight_sems, 0) + load_columns(ups, wu, weight_sems, 8)
    for load in weights:
        load.start()
    grad_load.wait()
    to_home = pltpu.make_async_copy(grad_buf, home_ref, grad_sems.at[1])

    @pl.when(jnp.logical_not(away))
    def _():
        to_home.start()
        to_home.wait()

    order = [flow.me] + [flow.places[s] for s in (3, 0, 1, 4, 5, 2, 6)]
    stores = []
    columns, width = wg.shape[1], wg.shape[0]

    def work(pair):
        both = pl.ds(2 * pair, 2)
        x = xs[both].reshape(-1, width)

        def tile(cols):
            gate = jnp.dot(x, wg[:, cols], preferred_element_type=wide)
            upward = jnp.dot(x, wu[:, cols], preferred_element_type=wide)
            sigma = jax.nn.sigmoid(gate)
            swish = gate * sigma
            shape = (2, -1, upward.shape[1])
            inner_s[both, :, cols] = (swish * upward).astype(low).reshape(shape)
            b_s[both, :, cols] = swish.astype(low).reshape(shape)
            factor = upward * sigma * (1.0 + gate * (1.0 - sigma))
            a_s[both, :, cols] = factor.astype(low).reshape(shape)

        tile(slice(None))
        for i in (2 * pair, 2 * pair + 1):
            place = order[i]
            for j, (buf, target) in enumerate(
                ((xs, all_ref), (inner_s, inner_ref), (a_s, a_ref), (b_s, b_ref))
            ):
                store = pltpu.make_async_copy(buf.at[i], target.at[place], store_sems.at[i, j])
                store.start()
                stores.append(store)

    own_load.wait()
    flow.take(3)
    wait_all(weights)
    work(0)
    flow.take_near()
    flow.take_side()
    beside.wait(slice(0, 1))
    grad_flow.begin(None)
    home_load = pltpu.make_async_copy(home_ref, grad_buf, grad_sems.at[2])
    home_load.start()
    work(1)
    home_load.wait()
    own_store = pltpu.make_async_copy(grad_buf, grads_ref.at[grad_flow.me], grad_sems.at[3])
    own_store.start()
    flow.take(4)
    flow.take(5)
    work(2)
    flow.take_far()
    grad_flow.take_near()
    grad_flow.take_side()
    flow.take(6)
    work(3)
    grad_flow.take_far()
    for slot in (3, 4, 5, 6):
        grad_flow.take(slot)
    flow.end()
    grad_flow.end()
    wait_all(stores + [own_store])
    beside.wait(slice(1, 5))


def feed_forward(own, gates, ups, downs, grad, number):
    count, width = own.shape
    columns = gates[0].shape[1]
    chunks = 4 if count % 64 == 0 else 1
    row, part = (8, count, width), (8, count, columns)
    sem = pltpu.SemaphoreType.DMA
    flops = 2 * 8 * count * width * columns * 2
    args = [own, *gates, *ups, *downs, grad]
    shapes = [row, part, part, part] + [a.shape for a in downs] + [grad.shape, row]
    return pl.pallas_call(
        functools.partial(feed_kernel, False, chunks),
        in_specs=[in_hbm()] * len(args),
        out_specs=[in_hbm()] * len(shapes),
        out_shape=[jax.ShapeDtypeStruct(s, low) for s in shapes],
        scratch_shapes=[
            pltpu.VMEM(row, low),
            pltpu.VMEM((width, columns), low),
            pltpu.VMEM((width, columns), low),
            pltpu.VMEM(part, low),
            pltpu.VMEM(part, low),
            pltpu.VMEM(part, low),
            pltpu.VMEM(grad.shape, low),
            sem((7, chunks)),
            sem((7, chunks)),
            sem((7, chunks)),
            sem((7, chunks)),
            sem((16,)),
            sem((8, 4)),
            sem,
            sem((2, 5)),
            sem((4,)),
        ],
        compiler_params=pltpu.CompilerParams(
            collective_id=number, has_side_effects=True, vmem_limit_bytes=56 * 1024 * 1024
        ),
        cost_estimate=pl.CostEstimate(
            flops=flops, bytes_accessed=100 * 1024 * 1024, transcendentals=0
        ),
        name="feed_forward",
    )(*args)


def feed_back_kernel(
    even, chunks, *refs,
):
    grad_ref, a_ref, b_ref, inner_ref, all_ref = refs[:5]
    gates, ups, downs, refs = refs[5:13], refs[13:21], refs[21:29], refs[29:]
    out_ref, terms_own, terms_twin, gate_own, gate_across, up_own, up_across = refs[:7]
    down_sum, down_across, down_came, refs = refs[7], refs[8], refs[9], refs[10:]
    down_own, down_stage, came_h, refs = refs[0], refs[1], refs[2], refs[3:]
    gx, wg, wu, wd, a_s, b_s, inner_s, terms_s, own_buf, twin_buf, twin_out, down_s = refs[:12]
    far_out, side_out, near_out, far_in, side_in, near_in = refs[12:18]
    sends, recvs, weight_sems, down_sems, block_sems, all_sems, terms_sems, more_sems = refs[18:]
    over_x, over_h = {"x": other(lax.axis_index("x"))}, {"h": other(lax.axis_index("h"))}
    at_h = lax.axis_index("h")
    halves_at = [pl.ds(0, grad_ref.shape[2] // 2), pl.ds(grad_ref.shape[2] // 2, grad_ref.shape[2] // 2)]
    steps_x = [
        remote(down_across.at[:, s], down_came.at[:, s], more_sems.at[0, i], more_sems.at[1, i], over_x)
        for i, s in enumerate(halves_at)
    ]
    steps_h = []

    def down_step(i):
        s = halves_at[i]
        steps_x[i].wait_recv()
        take = pltpu.make_async_copy(down_came.at[:, s], down_stage, more_sems.at[2, i])
        take.start()
        take.wait()
        total = down_own[:, s].astype(wide) + down_stage[...].astype(wide)
        down_own[:, s] = total.astype(low)
        part_rows = came_h.shape[0]
        theirs = down_own.at[pl.ds(pl.multiple_of(other(at_h) * part_rows, 16), part_rows), s]
        copy = remote(theirs, came_h.at[:, s], more_sems.at[0, 2 + i], more_sems.at[1, 2 + i], over_h)
        copy.start()
        steps_h.append(copy)

    c, l, y, near, side, twin = row_peers(even)
    rows = out_ref.shape[0] // chunks
    columns, width = wd.shape
    used = 4 * downs[0].shape[0]
    me = l * 2 + y
    near_at, side_at = near["l"] * 2 + near["y"], side["l"] * 2 + side["y"]
    far_at = other(l) * 2 + other(y)
    own_order = (far_at, side_at, near_at, me)
    twin_order = (far_at, near_at, side_at, me) if even else own_order
    pairs = []
    for p, q in zip(twin_order, own_order):
        pairs += [(other(c) * 4 + p, p, True), (c * 4 + q, q, False)]
    downs = load_rows((downs[:4], downs[4:]), wd, down_sems)
    blocks = []
    for i, (place, _, _) in enumerate(pairs):
        loads = [
            pltpu.make_async_copy(source.at[place], buf.at[i], block_sems.at[i, j])
            for j, (source, buf) in enumerate(
                ((grad_ref, gx), (a_ref, a_s), (b_ref, b_s), (inner_ref, inner_s))
            )
        ]
        for load in loads:
            load.start()
        blocks.append(loads)
    weights = load_columns(gates, wg, weight_sems, 0) + load_columns(ups, wu, weight_sems, 8)
    for load in weights:
        load.start()
    wd[used:, :] = jnp.zeros((columns - used, width), low)
    greet([near, side, twin, over_x, over_h])
    copies = []

    def start(source, target, slot, k, peer):
        copy = remote(source, target, sends.at[slot, k], recvs.at[slot, k], peer)
        copy.start()
        copies.append(copy)

    def arrived(slot, k):
        span = far_in.at[pl.ds(k * rows, rows)]
        remote(span, span, sends.at[slot, k], recvs.at[slot, k], twin).wait_recv()

    def block_arrived(slot):
        remote(
            own_buf.at[0], twin_buf.at[0], sends.at[slot, 0], recvs.at[slot, 0], twin
        ).wait_recv()

    def term(pair, twin_target, own_target):
        span = pl.ds(2 * pair, 2)
        grads = gx[span].reshape(-1, width)

        dinner = contract(grads, wd[...], ((1,), (1,))).reshape(2, -1, columns)
        a_s[span] = (dinner * a_s[span].astype(wide)).astype(low)
        b_s[span] = (dinner * b_s[span].astype(wide)).astype(low)
        if pair == 0:
            wait_all(weights)
        dgate = a_s[span].reshape(-1, columns)
        dup = b_s[span].reshape(-1, columns)

        def second(cols):
            part = contract(dgate, wg[cols, :], ((1,), (1,)))
            part = (part + contract(dup, wu[cols, :], ((1,), (1,)))).astype(low)
            half = part.shape[0] // 2
            twin_target[:, cols] = part[:half]
            own_target[:, cols] = part[half:]

        for_tiles(width, width // 2, second)

    def both(place, span):
        return own_buf[place, span, :].astype(wide) + twin_buf[place, span, :].astype(wide)

    spans = [(k, pl.ds(k * rows, rows)) for k in range(chunks)]
    for loads in blocks:
        wait_all(loads)
    inners = inner_s[...].reshape(-1, columns)
    x_at = lax.axis_index("x")
    down_rows = down_own.shape[0]

    def down_tile(j):
        span = slice(j * (width // 4), (j + 1) * (width // 4))
        part = contract(inners, gx[:, :, span].reshape(-1, width // 4), ((0,), (0,))).astype(low)
        down_s[...] = part
        at = pl.multiple_of(x_at * down_rows, 16)
        down_own[:, span] = down_s[pl.ds(at, down_rows), :]
        at = pl.multiple_of(other(x_at) * down_rows, 16)
        down_across[:, span] = down_s[pl.ds(at, down_rows), :]

    for j in range(4):
        down_tile(j)
        if j % 2:
            steps_x[j // 2].start()
    wait_all(downs)
    for i in range(4):
        twin_place, own_place = pairs[2 * i][1], pairs[2 * i + 1][1]
        term(i, twin_out.at[i], own_buf.at[own_place])
        start(twin_out.at[i], twin_buf.at[twin_place], 3 + i, 0, twin)
        if i >= 1:
            block_arrived(2 + i)
        if i == 1:
            for k, span in spans:
                far_out[span, :] = both(far_at, span).astype(low)
                start(far_out.at[span], far_in.at[span], 0, k, side)
        if i == 2:
            down_step(0)
            for k, span in spans:
                side_out[span, :] = both(side_at, span).astype(low)
                start(side_out.at[span], side_in.at[span], 1, k, side)
    block_arrived(6)
    all_loads = [
        pltpu.make_async_copy(all_ref.at[pairs[i][0]], gx.at[i], all_sems.at[i]) for i in range(8)
    ]
    for load in all_loads:
        load.start()
    stores = []

    def output_term(pair):
        span = pl.ds(2 * pair, 2)
        if pair:
            wait_all(stores[2 * pair - 2 :])
        inner = inner_s[span].reshape(-1, columns)

        def tile(cols):
            part = jnp.dot(inner, wd[:, cols], preferred_element_type=wide)
            terms_s[:, :, cols] = part.astype(low).reshape(2, -1, width // 2)

        for_tiles(width, width // 2, tile)
        for i in range(2):
            _, place, is_twin = pairs[2 * pair + i]
            store = pltpu.make_async_copy(
                terms_s.at[i],
                (terms_twin if is_twin else terms_own).at[place],
                terms_sems.at[2 * pair + i],
            )
            store.start()
            stores.append(store)

    for i in range(2):
        output_term(i)
    for k, span in spans:
        arrived(0, k)
        near_out[span, :] = (both(near_at, span) + far_in[span, :].astype(wide)).astype(low)
        start(near_out.at[span], near_in.at[span], 2, k, near)
    down_step(1)
    for i in range(2, 4):
        output_term(i)
    wait_all(all_loads)
    dgates = a_s[...].reshape(-1, columns)
    dups = b_s[...].reshape(-1, columns)

    half = width // 2
    for gate_ref, up_ref, at in ((gate_across, up_across, other(x_at)), (gate_own, up_own, x_at)):
        for j in range(2):
            cols = pl.ds(pl.multiple_of(at * half + j * (half // 2), 128), half // 2)
            rows_out = slice(j * (half // 2), (j + 1) * (half // 2))
            x = gx[:, :, cols].reshape(-1, half // 2)
            gate_ref[rows_out, :] = contract(x, dgates, ((0,), (0,))).astype(low)
            up_ref[rows_out, :] = contract(x, dups, ((0,), (0,))).astype(low)
    for k, span in spans:
        arrived(1, k)
        arrived(2, k)
        out_ref[span, :] = (
            both(me, span) + side_in[span, :].astype(wide) + near_in[span, :].astype(wide)
        )
    wait_all(stores[6:])
    for copy in steps_h:
        copy.wait()
    part_rows = came_h.shape[0]
    mine = down_own[pl.ds(pl.multiple_of(at_h * part_rows, 16), part_rows), :]
    down_sum[...] = mine.astype(wide) + came_h[...].astype(wide)
    for copy in copies + steps_x:
        copy.wait_send()


def feed_back(grad_all, a, b, inner, all_two, gate_pieces, up_pieces, down_parts, number):
    count, width = a.shape[1], all_two.shape[2]
    columns = a.shape[2]
    chunks = 4 if count % 64 == 0 else 1
    row, part = (8, count, width), (8, count, columns)
    sem = pltpu.SemaphoreType.DMA
    block = pltpu.VMEM((count, width), low)
    vmem = pl.BlockSpec(memory_space=pltpu.VMEM)
    flops = 2 * 8 * count * width * columns * 6
    args = [grad_all.reshape(row), a, b, inner, all_two, *gate_pieces, *up_pieces]
    args += [piece for parts in down_parts for piece in parts]
    own_rows = down_parts[0][0].shape[0]
    return pl.pallas_call(
        functools.partial(feed_back_kernel, True, chunks),
        in_specs=[in_hbm()] * len(args),
        out_specs=[vmem, in_hbm(), in_hbm()] + [vmem] * 6 + [in_hbm()],
        out_shape=[jax.ShapeDtypeStruct((count, width), wide)]
        + [jax.ShapeDtypeStruct((4, count, width), low)] * 2
        + [jax.ShapeDtypeStruct((width // 2, columns), low)] * 4
        + [jax.ShapeDtypeStruct((own_rows, width), wide)]
        + [jax.ShapeDtypeStruct((2 * own_rows, width), low)] * 2,
        scratch_shapes=[
            pltpu.VMEM((2 * own_rows, width), low),
            pltpu.VMEM((2 * own_rows, width // 2), low),
            pltpu.VMEM((own_rows, width), low),
            pltpu.VMEM(row, low),
            pltpu.VMEM((width, columns), low),
            pltpu.VMEM((width, columns), low),
            pltpu.VMEM((columns, width), low),
            pltpu.VMEM(part, low),
            pltpu.VMEM(part, low),
            pltpu.VMEM(part, low),
            pltpu.VMEM((2, count, width), low),
            pltpu.VMEM((4, count, width), low),
            pltpu.VMEM((4, count, width), low),
            pltpu.VMEM((4, count, width), low),
            pltpu.VMEM((columns, width // 4), low),
        ]
        + [block] * 6
        + [
            sem((7, chunks)),
            sem((7, chunks)),
            sem((16,)),
            sem((8,)),
            sem((8, 4)),
            sem((8,)),
            sem((8,)),
            sem((3, 4)),
        ],
        compiler_params=pltpu.CompilerParams(
            collective_id=number, has_side_effects=True, vmem_limit_bytes=60 * 1024 * 1024
        ),
        cost_estimate=pl.CostEstimate(
            flops=flops, bytes_accessed=100 * 1024 * 1024, transcendentals=0
        ),
        name="feed_back",
    )(*args)


def scatter_kernel(even, chunks, n, kinds, *refs):
    m = len(kinds)
    terms, more, refs = refs[:n], refs[n : n + m], refs[n + m :]
    outs, more_out, refs = refs[:n], refs[n : n + m], refs[n + m :]
    bufs, (sends, recvs, local_sems, more_sems) = refs[: 8 * n], refs[8 * n :]
    beside = Beside(kinds, more, more_out, more_sems)
    bufs = [bufs[8 * a : 8 * a + 8] for a in range(n)]
    c, l, y, near, side, twin = row_peers(even)
    rows = outs[0].shape[0] // chunks
    me = l * 2 + y
    near_at, side_at = near["l"] * 2 + near["y"], side["l"] * 2 + side["y"]
    far_at = other(l) * 2 + other(y)
    greet([near, side, twin] + beside.peers)
    beside.start()
    copies = []

    def start(source, target, a, slot, k, peer):
        copy = remote(source, target, sends.at[a, slot, k], recvs.at[a, slot, k], peer)
        copy.start()
        copies.append(copy)

    parts = [(a, k, pl.ds(k * rows, rows)) for k in range(chunks) for a in range(n)]
    twin_side, twin_near = (near_at, side_at) if even else (side_at, near_at)
    for slot, place in ((3, far_at), (4, twin_side), (5, twin_near), (6, me)):
        for a, k, span in parts:
            start(
                terms[a].at[other(c) * 4 + place, span], bufs[a][1].at[place, span], a, slot, k, twin
            )
    loads = []
    for slot, place in ((0, far_at), (1, side_at), (2, near_at), (3, me)):
        for a in range(n):
            load = pltpu.make_async_copy(
                terms[a].at[c * 4 + place], bufs[a][0].at[place], local_sems.at[a, slot]
            )
            load.start()
            loads.append(load)

    def arrived(a, slot, k):
        span = bufs[a][5].at[pl.ds(k * rows, rows)]
        remote(span, span, sends.at[a, slot, k], recvs.at[a, slot, k], twin).wait_recv()

    def both(a, place, span):
        own, came = bufs[a][0], bufs[a][1]
        return own[place, span, :].astype(wide) + came[place, span, :].astype(wide)

    for load in loads[: 2 * n]:
        load.wait()
    for a, k, span in parts:
        far_out, far_in = bufs[a][2], bufs[a][5]
        arrived(a, 3, k)
        far_out[span, :] = both(a, far_at, span).astype(low)
        start(far_out.at[span], far_in.at[span], a, 0, k, side)
    for a, k, span in parts:
        side_out, side_in = bufs[a][3], bufs[a][6]
        arrived(a, 4, k)
        side_out[span, :] = both(a, side_at, span).astype(low)
        start(side_out.at[span], side_in.at[span], a, 1, k, side)
    for load in loads[2 * n :]:
        load.wait()
    for a, k, span in parts:
        near_out, far_in, near_in = bufs[a][4], bufs[a][5], bufs[a][7]
        arrived(a, 5, k)
        arrived(a, 0, k)
        near_out[span, :] = (both(a, near_at, span) + far_in[span, :].astype(wide)).astype(low)
        start(near_out.at[span], near_in.at[span], a, 2, k, near)
    for a, k, span in parts:
        arrived(a, 6, k)
        arrived(a, 1, k)
        outs[a][span, :] = both(a, me, span) + bufs[a][6][span, :].astype(wide)
    for a, k, span in parts:
        arrived(a, 2, k)
        outs[a][span, :] += bufs[a][7][span, :].astype(wide)
    for copy in copies:
        copy.wait_send()
    beside.wait()


def scatter_row(number, *terms, even=False, kinds=(), more=()):
    if lax.axis_size("l") != 2:
        return [
            lax.psum_scatter(t.astype(wide), group, scatter_dimension=0, tiled=True) for t in terms
        ]
    terms = [t.reshape(8, -1, t.shape[1]) for t in terms]
    n, count = len(terms), terms[0].shape[1]
    chunks = 4 if count % 64 == 0 else 1
    scratch = []
    for t in terms:
        scratch += [pltpu.VMEM((4, count, t.shape[2]), low)] * 2
        scratch += [pltpu.VMEM((count, t.shape[2]), low)] * 6
    return pl.pallas_call(
        functools.partial(scatter_kernel, even, chunks, n, kinds),
        in_specs=[in_hbm()] * (n + len(more)),
        out_specs=[pl.BlockSpec(memory_space=pltpu.VMEM)] * n + [in_hbm()] * len(more),
        out_shape=[jax.ShapeDtypeStruct((count, t.shape[2]), wide) for t in terms]
        + [jax.ShapeDtypeStruct(a.shape, low) for a in more],
        scratch_shapes=scratch
        + [
            pltpu.SemaphoreType.DMA((n, 7, chunks)),
            pltpu.SemaphoreType.DMA((n, 7, chunks)),
            pltpu.SemaphoreType.DMA((n, 4)),
            pltpu.SemaphoreType.DMA((2, max(1, len(more)))),
        ],
        compiler_params=pltpu.CompilerParams(
            collective_id=number, has_side_effects=True, vmem_limit_bytes=24 * 1024 * 1024
        ),
        cost_estimate=pl.CostEstimate(flops=0, bytes_accessed=80 * 1024 * 1024, transcendentals=0),
        name="scatter_row",
    )(*terms, *more)


class SumColumns:
    def __init__(self, mine_ref, across_ref, land_ref, out_ref, mine, stage, came_h, sems, local_sems):
        self.h = lax.axis_index("h")
        over_x, self.over_h = {"x": other(lax.axis_index("x"))}, {"h": other(self.h)}
        self.land_ref, self.out_ref = land_ref, out_ref
        self.mine, self.stage, self.came_h = mine, stage, came_h
        self.sems, self.local_sems = sems, local_sems
        rows = mine.shape[2] // 2
        self.parts = [(c, pl.ds(i * rows, rows)) for c in range(2) for i in range(2)]
        self.steps_x = [
            remote(
                across_ref.at[c, :, s], land_ref.at[c, :, s], sems.at[0, i], sems.at[1, i], over_x
            )
            for i, (c, s) in enumerate(self.parts)
        ]
        self.steps_h = []
        self.load = pltpu.make_async_copy(mine_ref, mine, local_sems.at[0])

    def start(self):
        for copy in self.steps_x:
            copy.start()
        self.load.start()

    def step(self, i):
        c, s = self.parts[i]
        if i == 0:
            self.load.wait()
        self.steps_x[i].wait_recv()
        take = pltpu.make_async_copy(self.land_ref.at[c, :, s], self.stage, self.local_sems.at[1])
        take.start()
        take.wait()
        total = self.mine[c, :, s].astype(wide) + self.stage[...].astype(wide)
        self.mine[c, :, s] = total.astype(low)
        copy = remote(
            self.mine.at[c, other(self.h), s], self.came_h.at[c, s], self.sems.at[0, 4 + i],
            self.sems.at[1, 4 + i], self.over_h,
        )
        copy.start()
        self.steps_h.append(copy)

    def end(self):
        for (c, s), copy in zip(self.parts, self.steps_h):
            copy.wait()
            total = self.mine[c, self.h, s].astype(wide) + self.came_h[c, s].astype(wide)
            self.out_ref[c, s] = total.astype(low)
        for copy in self.steps_x:
            copy.wait_send()


def middle_kernel(heads, tile, scale, chunks, *refs):
    ends_ref, branch_ref, gate_mine, gate_across, up_mine, up_across, terms_own, terms_twin = refs[:8]
    query_ref, mixed_ref, packed_ref, logs_ref, cos_in, sin_in, out_in, up_in = refs[8:16]
    resid_ref, refs = refs[16], refs[17:]
    dlow_out, dkv_out, gate_out, up_out, final_ref, by_h_ref, head_out = refs[:7]
    land_gate, land_up, land_twin, refs = *refs[7:10], refs[10:]
    xs, kv, q, o, logs, cos_ref, sin_ref, out_own, up_query, dq, dlow, dkv_sum, dkv = refs[:13]
    refs = refs[13:]
    scatter_bufs, refs = (refs[:7], refs[7:14]), refs[14:]
    stage_a, stage_b, stage_c, sp_far, sp_side, sp_near, sp_far_in, sp_side_in, sp_near_in = refs[:9]
    refs = refs[9:]
    gate_own, gate_h, up_own, up_h, column_stage, refs = *refs[:5], refs[5:]
    go, came_o, came_y, gh, came_hx, came_hh, refs = *refs[:6], refs[6:]
    sends, recvs, sc_sends, sc_recvs, sp_sems, gate_sems, up_sems = refs[:7]
    chain_sems, load_sems, block_sems, local_sems = refs[7:]
    x, h, y_at = [lax.axis_index(a) for a in ("x", "h", "y")]
    c, l, y, near, side, twin = row_peers(False)
    count = branch_ref.shape[0]
    rows = count // chunks
    width = up_query.shape[1] // heads
    half, low_width = width // 2, up_query.shape[0]
    over_x, over_h, over_y = {"x": other(x)}, {"h": other(h)}, {"y": other(y)}
    me = l * 2 + y
    near_at, side_at = near["l"] * 2 + near["y"], side["l"] * 2 + side["y"]
    far_at = other(l) * 2 + other(y)
    flow = RowGather(True, chunks, branch_ref, xs, sends, recvs)
    gate = SumColumns(
        gate_mine, gate_across, land_gate, gate_out, gate_own, column_stage, gate_h, gate_sems,
        local_sems.at[0],
    )
    up = SumColumns(
        up_mine, up_across, land_up, up_out, up_own, column_stage, up_h, up_sems, local_sems.at[1]
    )
    greet([near, side, twin, over_x, over_h])
    flow.begin(None)
    sp_twin = remote(terms_twin, land_twin, sp_sems.at[0, 0], sp_sems.at[1, 0], twin)
    sp_twin.start()
    gate.start()
    up.start()
    own_load = pltpu.make_async_copy(branch_ref, xs.at[flow.me], load_sems.at[0])
    own_load.start()
    loads = [
        pltpu.make_async_copy(source, target, load_sems.at[1 + i])
        for i, (source, target) in enumerate(
            (
                (packed_ref.at[:, pl.ds(low_width, 2 * width)], kv), (query_ref, q), (mixed_ref, o),
                (logs_ref, logs), (cos_in, cos_ref), (sin_in, sin_ref), (out_in, out_own),
                (up_in, up_query),
            )
        )
    ]
    for load in loads:
        load.start()

    sp_copies = [sp_twin]

    def sp_pair(place):
        first = pltpu.make_async_copy(terms_own.at[place], stage_a, local_sems.at[2, 0])
        second = pltpu.make_async_copy(land_twin.at[place], stage_b, local_sems.at[2, 1])
        first.start()
        second.start()
        first.wait()
        second.wait()
        return stage_a[...].astype(wide) + stage_b[...].astype(wide)

    def sp_send(total, buf, target, slot, peer):
        buf[...] = total.astype(low)
        copy = remote(buf, target, sp_sems.at[0, slot], sp_sems.at[1, slot], peer)
        copy.start()
        sp_copies.append(copy)

    def sp_arrived(slot):
        remote(sp_far, sp_far_in, sp_sems.at[0, slot], sp_sems.at[1, slot], twin).wait_recv()

    dkv_sum[...] = jnp.zeros_like(dkv_sum)
    flow.take_near()
    gate.step(0)
    flow.take_side()
    sp_twin.wait_recv()
    sp_send(sp_pair(far_at), sp_far, sp_far_in, 1, side)
    sp_send(sp_pair(side_at), sp_side, sp_side_in, 2, side)
    gate.step(1)
    flow.take(3)
    flow.take(4)
    gate.step(2)
    flow.take_far()
    flow.take(5)
    gate.step(3)
    flow.take(6)
    own_load.wait()
    wait_all(loads)

    def grad_out(at):
        cols = pl.ds(pl.multiple_of(at * 256, 256), 256)
        for j in range(2):
            span = slice(j * 1024, (j + 1) * 1024)
            branch = xs[:, :, span].reshape(-1, 1024)
            go[at, :, span] = contract(o[:, cols], branch, ((0,), (0,))).astype(low)

    grad_out(other(x))
    out_x = remote(go.at[other(x)], came_o, chain_sems.at[0, 0], chain_sems.at[1, 0], over_x)
    out_x.start()
    grad_out(x)

    def block_rows(begin, size):
        first, offset = begin // count, begin % count
        got = min(size, count - offset)
        parts = [xs[first, offset : offset + got, :]]
        if got < size:
            parts.append(xs[first + 1, : size - got, :])
        return jnp.concatenate(parts, axis=0) if len(parts) > 1 else parts[0]

    def attention(i):
        span, length = slice(i * tile, (i + 1) * tile), (i + 1) * tile
        mask = tile_mask(ends_ref, i * tile, tile, length, heads)
        queries = stacked(q, span, heads, width)
        dmixed = contract(block_rows(i * tile, tile), out_own[...], ((1,), (1,))).astype(low)
        grads = jnp.concatenate(
            [dmixed[:, j * width : (j + 1) * width] for j in range(heads)], axis=0
        )
        outs = stacked(o, span, heads, width)
        delta = jnp.sum(grads.astype(wide) * outs.astype(wide), axis=1, keepdims=True)
        log = jnp.concatenate([logs[j, span, :1] for j in range(heads)], axis=0)
        keys, values = kv[:length, :width], kv[:length, width:]
        scores = contract(queries, keys, ((1,), (1,)))
        weights = jnp.where(mask, jnp.exp(scores - log), 0.0)
        dprob = contract(grads, values, ((1,), (1,)))
        dscore = (weights * (dprob - delta)).astype(low)
        dkv_sum[:length, width:] += contract(weights.astype(low), grads, ((0,), (0,)))
        dkv_sum[:length, :width] += contract(dscore, queries, ((0,), (0,)))
        dquery = contract(dscore, keys, ((1,), (0,))) * scale
        cosine, sine = cos_ref[span, :], sin_ref[span, :]
        for j in range(heads):
            a = dquery[j * tile : (j + 1) * tile, :half]
            b = dquery[j * tile : (j + 1) * tile, half:]
            at = j * width
            dq[span, at : at + half] = (a * cosine + b * sine).astype(low)
            dq[span, at + half : at + width] = (b * cosine - a * sine).astype(low)
        dlow[span, :] = contract(dq[span, :], up_query[...], ((1,), (1,))).astype(low)

    for i in range(q.shape[0] // tile):
        attention(i)
        if i == 3:
            up.step(0)
        if i == 4:
            sp_arrived(1)
            sp_send(
                sp_pair(near_at) + sp_far_in[...].astype(wide), sp_near, sp_near_in, 3, near
            )
    dkv[...] = dkv_sum[...].astype(low)
    flow.end()
    latents = [
        pltpu.make_async_copy(
            packed_ref.at[pl.ds(i * count, count), pl.ds(0, low_width)],
            xs.at[i, :, pl.ds(0, low_width)],
            block_sems.at[i],
        )
        for i in range(8)
    ]
    for load in latents:
        load.start()

    sc_copies = []
    terms = (dlow, dkv)
    sc_parts = [(a, k, pl.ds(k * rows, rows)) for k in range(chunks) for a in range(2)]

    def sc_start(source, target, a, slot, k, peer):
        copy = remote(source, target, sc_sends.at[a, slot, k], sc_recvs.at[a, slot, k], peer)
        copy.start()
        sc_copies.append(copy)

    def sc_arrived(a, slot, k):
        span = scatter_bufs[a][4].at[pl.ds(k * rows, rows)]
        remote(span, span, sc_sends.at[a, slot, k], sc_recvs.at[a, slot, k], twin).wait_recv()

    def term_rows(core, place, k):
        return pl.ds(pl.multiple_of((core * 4 + place) * count + k * rows, 16), rows)

    for slot, place in ((3, far_at), (4, side_at), (5, near_at), (6, me)):
        for a, k, span in sc_parts:
            sc_start(
                terms[a].at[term_rows(other(c), place, k)], scatter_bufs[a][0].at[place, span], a,
                slot, k, twin,
            )

    up.step(1)

    def both(a, place, k, span):
        own = terms[a][term_rows(c, place, k), :]
        return own.astype(wide) + scatter_bufs[a][0][place, span, :].astype(wide)

    for a, k, span in sc_parts:
        far_out, far_in = scatter_bufs[a][1], scatter_bufs[a][4]
        sc_arrived(a, 3, k)
        far_out[span, :] = both(a, far_at, k, span).astype(low)
        sc_start(far_out.at[span], far_in.at[span], a, 0, k, side)
    up.step(2)
    for a, k, span in sc_parts:
        side_out, side_in = scatter_bufs[a][2], scatter_bufs[a][5]
        sc_arrived(a, 4, k)
        side_out[span, :] = both(a, side_at, k, span).astype(low)
        sc_start(side_out.at[span], side_in.at[span], a, 1, k, side)
    wait_all(latents)
    dqs = dq[...]

    def grad_heads(at):
        cols = pl.ds(pl.multiple_of(at * (low_width // 2), 128), low_width // 2)
        latent = xs[:, :, cols].reshape(-1, low_width // 2)
        gh[at] = contract(latent, dqs, ((0,), (0,))).astype(low).reshape(gh.shape[1:])

    grad_heads(other(x))
    head_x = remote(gh.at[other(x)], came_hx, chain_sems.at[0, 1], chain_sems.at[1, 1], over_x)
    head_x.start()
    grad_heads(x)
    up.step(3)
    for a, k, span in sc_parts:
        near_out, far_in, near_in = scatter_bufs[a][3], scatter_bufs[a][4], scatter_bufs[a][6]
        sc_arrived(a, 5, k)
        sc_arrived(a, 0, k)
        near_out[span, :] = (both(a, near_at, k, span) + far_in[span, :].astype(wide)).astype(low)
        sc_start(near_out.at[span], near_in.at[span], a, 2, k, near)
    out_x.wait_recv()
    total = go[x].astype(wide) + came_o[...].astype(wide)
    go[x] = total.astype(low)
    part = by_h_ref.shape[1]
    mine_rows = pl.ds(pl.multiple_of(y * part, part), part)
    their_rows = pl.ds(pl.multiple_of(other(y) * part, part), part)
    out_y = remote(
        go.at[x, their_rows], came_y, chain_sems.at[0, 2], chain_sems.at[1, 2], over_y
    )
    out_y.start()
    head_x.wait_recv()
    gh[x] = (gh[x].astype(wide) + came_hx[...].astype(wide)).astype(low)
    head_h = remote(
        gh.at[x, :, other(h)], came_hh, chain_sems.at[0, 3], chain_sems.at[1, 3], over_h
    )
    head_h.start()
    sp_arrived(2)
    sp_arrived(3)
    resid_load = pltpu.make_async_copy(resid_ref, stage_c, local_sems.at[2, 0])
    resid_load.start()
    resid_load.wait()
    total = sp_pair(me) + sp_side_in[...].astype(wide) + sp_near_in[...].astype(wide)
    final_ref[...] = (stage_c[...] + total).astype(low)
    gate.end()
    outs = (dlow_out, dkv_out)
    for a, k, span in sc_parts:
        sc_arrived(a, 6, k)
        sc_arrived(a, 1, k)
        outs[a][span, :] = both(a, me, k, span) + scatter_bufs[a][5][span, :].astype(wide)
    for a, k, span in sc_parts:
        sc_arrived(a, 2, k)
        outs[a][span, :] += scatter_bufs[a][6][span, :].astype(wide)
    by_h_ref[y] = go[x, mine_rows, :]
    out_y.wait_recv()
    by_h_ref[other(y)] = came_y[...]
    head_h.wait_recv()
    head_out[...] = (gh[x, :, h].astype(wide) + came_hh[...].astype(wide)).astype(low)
    up.end()
    for copy in sp_copies + sc_copies + [out_x, out_y, head_x, head_h]:
        copy.wait_send()


def middle(
    ends, branch, gate_terms, up_terms, spread, query, mixed, packed, logs, cosine, sine, out_own,
    up_query, resid, heads, scale, number,
):
    count, width = branch.shape
    length, columns = query.shape
    low_width = up_query.shape[0]
    chunks = 4
    args = [
        ends, branch, *gate_terms, *up_terms, *spread, query, mixed, packed, logs, cosine, sine,
        out_own, up_query, resid,
    ]
    kept = (2,) + gate_terms[0].shape[2:]
    part = columns // 4
    rows_up = low_width // 8
    vmem, sem = pl.BlockSpec(memory_space=pltpu.VMEM), pltpu.SemaphoreType.DMA
    shapes = [
        ((count, low_width), wide),
        ((count, columns), wide),
        (kept, low),
        (kept, low),
        ((count, width), low),
        ((2, part, width), low),
        ((2, rows_up, columns), low),
        (gate_terms[0].shape, low),
        (up_terms[0].shape, low),
        (spread[0].shape, low),
    ]
    block = pltpu.VMEM((count, width), low)

    def scatter_scratch(w):
        return [pltpu.VMEM((4, count, w), low)] + [pltpu.VMEM((count, w), low)] * 6

    return pl.pallas_call(
        functools.partial(middle_kernel, heads, tile_of(length), scale, chunks),
        in_specs=[pl.BlockSpec(memory_space=pltpu.SMEM)] + [in_hbm()] * (len(args) - 1),
        out_specs=[vmem] * 7 + [in_hbm()] * 3,
        out_shape=[jax.ShapeDtypeStruct(*s) for s in shapes],
        scratch_shapes=[
            pltpu.VMEM((8, count, width), low),
            pltpu.VMEM((length, columns), low),
            pltpu.VMEM((length, columns), low),
            pltpu.VMEM((length, columns), low),
            pltpu.VMEM(logs.shape, wide),
            pltpu.VMEM(cosine.shape, wide),
            pltpu.VMEM(sine.shape, wide),
            pltpu.VMEM(out_own.shape, low),
            pltpu.VMEM(up_query.shape, low),
            pltpu.VMEM((length, columns), low),
            pltpu.VMEM((length, low_width), low),
            pltpu.VMEM((length, columns), wide),
            pltpu.VMEM((length, columns), low),
            *scatter_scratch(low_width),
            *scatter_scratch(columns),
            block,
            block,
            pltpu.VMEM((count, width), wide),
            *[block] * 6,
            pltpu.VMEM(gate_terms[0].shape, low),
            pltpu.VMEM(kept, low),
            pltpu.VMEM(up_terms[0].shape, low),
            pltpu.VMEM(kept, low),
            pltpu.VMEM((2, kept[1] // 2, kept[2]), low),
            pltpu.VMEM((2, columns // 2, width), low),
            pltpu.VMEM((columns // 2, width), low),
            pltpu.VMEM((part, width), low),
            pltpu.VMEM((2, 2, 2, rows_up, columns), low),
            pltpu.VMEM((2, 2, rows_up, columns), low),
            pltpu.VMEM((2, rows_up, columns), low),
            sem((7, chunks)),
            sem((7, chunks)),
            sem((2, 7, chunks)),
            sem((2, 7, chunks)),
            sem((2, 4)),
            sem((2, 8)),
            sem((2, 8)),
            sem((2, 4)),
            sem((9,)),
            sem((8,)),
            sem((3, 2)),
        ],
        compiler_params=pltpu.CompilerParams(
            collective_id=number, has_side_effects=True, vmem_limit_bytes=63 * 1024 * 1024
        ),
        cost_estimate=pl.CostEstimate(
            flops=18 * length * length * columns,
            bytes_accessed=200 * 1024 * 1024,
            transcendentals=length * length * heads // 2,
        ),
        name="middle",
    )(*args)


def norm_back_rows(incoming, source, gain):
    scale = rms_scale(source)
    weighted = incoming * gain
    mean = jnp.mean(weighted * source, axis=-1, keepdims=True)
    grad = scale * weighted - source * (scale * scale * scale) * mean
    return grad, jnp.sum(incoming * source * scale, axis=0, keepdims=True)


def shut_kernel(part, head_dim, order, n_in, n_out, *refs):
    ins, outs, refs = refs[:n_in], refs[n_in : n_in + n_out], refs[n_in + n_out :]
    (
        dlow_ref, dkv_ref, latent_ref, gain_latent_ref, cos_ref, sin_ref, hidden_ref, in_full_ref,
        home_ref, gain_one_ref, dresid_ref, gain_two_ref, gate_ref, up_ref, heads_ref, final_ref,
        kept_ref, across_ref,
    ) = ins
    sum_ref, tokens_ref, output_ref, gate_out, up_out, heads_out, out_ref = outs
    full, mapped, terms, gains, twin_buf, held, came, moved, swap_buf = refs[:9]
    gate_in, up_in, heads_in, final_buf, across_in = refs[9:14]
    sends, recvs, set_sends, set_recvs, swap_sems, local_sems = refs[14:]
    x, c, h, l, y = [lax.axis_index(a) for a in every]
    hops = {
        1: {"h": other(h)},
        2: {"l": other(l)},
        4: {"y": other(y)},
        8: {"x": other(x)},
    }
    twin = {"c": other(c)}
    cross = {"c": other(c), "h": other(h)}
    me = (c * 2 + l) * 2 + y

    def group_peer(k):
        return {"c": other(c, k // 4), "l": other(l, k // 2 % 2), "y": other(y, k % 2)}

    def group_index(k):
        peer = group_peer(k)
        return (peer["c"] * 2 + peer["l"]) * 2 + peer["y"]

    def index(code, core):
        at_x, at_l = other(x, code // 8 % 2), other(l, code // 2 % 2)
        return (((at_x * 2 + core) * 2 + other(h, code % 2)) * 2 + at_l) * 2 + other(y, code // 4 % 2)

    load = pltpu.make_async_copy(in_full_ref, full, local_sems.at[0])
    load.start()
    greet([hops[1], hops[8], cross] + [group_peer(k) for k in range(1, 8)])
    set_copies = []
    for i, (source, target) in enumerate(
        ((heads_ref, heads_in), (gate_ref, gate_in), (up_ref, up_in))
    ):
        for k in range(1, 8):
            copy = remote(
                source.at[group_index(k)], target.at[me], set_sends.at[i, k], set_recvs.at[i, k],
                group_peer(k),
            )
            copy.start()
            set_copies.append(copy)
    set_loads = [
        pltpu.make_async_copy(source.at[me], target.at[me], local_sems.at[1 + i])
        for i, (source, target) in enumerate(
            ((heads_ref, heads_in), (gate_ref, gate_in), (up_ref, up_in))
        )
    ]
    for copy in set_loads:
        copy.start()
    exchange = remote(across_ref, across_in, swap_sems.at[0], swap_sems.at[1], hops[1])
    output_move = remote(final_ref, output_ref, swap_sems.at[2], swap_sems.at[3], cross)
    tokens_move = remote(swap_buf, moved, swap_sems.at[4], swap_sems.at[5], cross)
    final_load = pltpu.make_async_copy(final_ref, final_buf, local_sems.at[4])
    final_store = pltpu.make_async_copy(final_buf, output_ref, local_sems.at[5])

    @pl.when(c != h)
    def _():
        output_move.start()

    @pl.when(c == h)
    def _():
        final_load.start()

    width, low_width = hidden_ref.shape[1], latent_ref.shape[1]
    half = head_dim // 2
    dlatent, dgain_latent = norm_back_rows(dlow_ref[...], latent_ref[...], gain_latent_ref[...])
    mapped[:, :low_width] = dlatent.astype(low)
    a, b = dkv_ref[:, :half], dkv_ref[:, half:head_dim]
    cosine, sine = cos_ref[...], sin_ref[...]
    mapped[:, low_width : low_width + half] = (a * cosine + b * sine).astype(low)
    mapped[:, low_width + half : low_width + head_dim] = (b * cosine - a * sine).astype(low)
    mapped[:, low_width + head_dim : low_width + 2 * head_dim] = dkv_ref[:, head_dim:].astype(low)
    mapped[:, low_width + 2 * head_dim :] = jnp.zeros((mapped.shape[0], 128), low)
    load.wait()
    dmapped = mapped[...]
    weights = full[...].reshape(width, -1)
    dhidden = contract(dmapped, weights, ((1,), (1,)))
    dinput, dgain_one = norm_back_rows(dhidden, home_ref[...].astype(wide), gain_one_ref[...])
    dtokens = dresid_ref[...] + dinput
    tokens_ref[...] = dtokens
    swap_buf[...] = dtokens.astype(low)

    gains[...] = jnp.zeros_like(gains)
    gains[0:1, :width] = dgain_one
    gains[1:2, :width] = gain_two_ref[...]
    gains[2:3, :low_width] = dgain_latent
    rows = terms.shape[1]
    low_part = low_width // 32
    used = low_width + 2 * head_dim
    for at in range(0, 32, 4):
        left = hidden_ref[:, at * rows : (at + 4) * rows]
        block = contract(left, dmapped[:, :used], ((0,), (0,))).astype(low)
        terms[at : at + 4, :, :used] = block.reshape(4, rows, used)
        for i in range(at, at + 4):
            tile = jnp.concatenate(
                [
                    gains[0:2, i * rows : i * rows + 128],
                    gains[2:3, i * low_part : i * low_part + 128],
                    jnp.zeros((rows - 3, 128), wide),
                ],
                axis=0,
            )
            terms[i, :, used:] = tile.astype(low)
    copies = []

    def start(source, target, slot, peer):
        copy = remote(source, target, sends.at[slot], recvs.at[slot], peer)
        copy.start()
        copies.append(copy)

    def arrived(slot):
        remote(came.at[0], came.at[0], sends.at[slot], recvs.at[slot], twin).wait_recv()

    for code in range(15, -1, -1):
        start(terms.at[index(code, 1 - c)], twin_buf.at[code], 16 + code, twin)
    for code in range(15, -1, -1):
        arrived(16 + code)
        total = terms[index(code, c)].astype(wide) + twin_buf[code].astype(wide)
        for hop in (8, 4, 2, 1):
            if code < hop:
                arrived(code + hop)
                total = total + came[code + hop].astype(wide)
        if code == 0:
            sum_ref[...] = total
        else:
            held[code] = total.astype(low)
            hop = 1 << (code.bit_length() - 1)
            start(held.at[code], came.at[code], code, hops[hop])
        if code == 8:

            @pl.when(c != h)
            def _():
                tokens_move.start()

            exchange.start()

        if code == 4:
            for copy in set_loads:
                copy.wait()
            for copy in set_copies:
                copy.wait()
            for source, target in ((gate_in, gate_out), (up_in, up_out)):
                for place, blocks in enumerate(order):
                    for j, block in enumerate(blocks):
                        target[:, block * part : (block + 1) * part] = source[
                            place, :, j * part : (j + 1) * part
                        ].astype(wide)
            for place in range(8):
                core, at_l, at_y = place // 4, place // 2 % 2, place % 2
                for j in range(2):
                    head = ((j * 2 + core) * 2 + at_y) * 2 + at_l
                    heads_out[:, head * head_dim : (head + 1) * head_dim] = heads_in[
                        place, :, j * head_dim : (j + 1) * head_dim
                    ].astype(wide)
    exchange.wait()
    out_ref[...] = kept_ref[...].astype(wide) + across_in[...].astype(wide)
    for copy in copies:
        copy.wait_send()

    @pl.when(c != h)
    def _():
        output_move.wait()
        tokens_move.wait()
        tokens_ref[...] = moved[...].astype(wide)

    @pl.when(c == h)
    def _():
        final_load.wait()
        final_store.start()
        final_store.wait()


def shut(
    dlow, dkv, latent, gain_latent, cosine, sine, hidden, in_full, home, gain_one, dresid, dgain_two,
    gate_terms, up_terms, head_terms, final, kept, across, part, order, number,
):
    count, width = hidden.shape
    head_dim = dkv.shape[1] // 2
    rows, columns = in_full.shape[1:]
    vmem, sem = pl.BlockSpec(memory_space=pltpu.VMEM), pltpu.SemaphoreType.DMA
    args = [
        dlow, dkv, latent, gain_latent, cosine, sine, hidden, in_full, home, gain_one, dresid,
        dgain_two, gate_terms, up_terms, head_terms, final, kept, across,
    ]
    hbm = {7, 12, 13, 14, 15, 17}
    ff = len(order) * len(order[0]) * part
    shapes = [
        ((rows, columns), wide),
        ((count, width), wide),
        ((count, width), low),
        ((gate_terms.shape[1], ff), wide),
        ((up_terms.shape[1], ff), wide),
        ((head_terms.shape[1], 8 * head_terms.shape[2]), wide),
        (kept.shape, wide),
    ]
    blocks = pltpu.VMEM((16, rows, columns), low)
    return pl.pallas_call(
        functools.partial(shut_kernel, part, head_dim, order, len(args), len(shapes)),
        in_specs=[in_hbm() if i in hbm else vmem for i in range(len(args))],
        out_specs=[in_hbm() if i == 2 else vmem for i in range(len(shapes))],
        out_shape=[jax.ShapeDtypeStruct(*s) for s in shapes],
        scratch_shapes=[
            pltpu.VMEM(in_full.shape, low),
            pltpu.VMEM((count, columns), low),
            pltpu.VMEM(in_full.shape, low),
            pltpu.VMEM((16, width + 128), wide),
            blocks,
            blocks,
            blocks,
            pltpu.VMEM((count, width), low),
            pltpu.VMEM((count, width), low),
            pltpu.VMEM(gate_terms.shape, low),
            pltpu.VMEM(up_terms.shape, low),
            pltpu.VMEM(head_terms.shape, low),
            pltpu.VMEM((count, width), low),
            pltpu.VMEM(across.shape, low),
            sem((32,)),
            sem((32,)),
            sem((3, 8)),
            sem((3, 8)),
            sem((6,)),
            sem((6,)),
        ],
        compiler_params=pltpu.CompilerParams(
            collective_id=number, has_side_effects=True, vmem_limit_bytes=60 * 1024 * 1024
        ),
        cost_estimate=pl.CostEstimate(flops=0, bytes_accessed=150 * 1024 * 1024, transcendentals=0),
        name="shut",
    )(*args)


def split_kernel(part, order, a_ref, b_ref, a_out, b_out):
    for source, target in ((a_ref, a_out), (b_ref, b_out)):
        used, total = len(order[0]) * part, target.shape[2]
        for place, blocks in enumerate(order):
            for j, block in enumerate(blocks):
                target[place, :, j * part : (j + 1) * part] = source[
                    :, block * part : (block + 1) * part
                ]
            if used < total:
                target[place, :, used:] = jnp.zeros((target.shape[1], total - used), target.dtype)


def join_kernel(part, order, a_ref, b_ref, a_out, b_out):
    for source, target in ((a_ref, a_out), (b_ref, b_out)):
        for place, blocks in enumerate(order):
            for j, block in enumerate(blocks):
                target[:, block * part : (block + 1) * part] = source[
                    place, :, j * part : (j + 1) * part
                ].astype(wide)


def column_order(n_x, n_l):
    return [
        [
            (((x * 2 + c) * 2 + h) * n_l + l) * 2 + y
            for x in range(n_x)
            for h in range(2)
        ]
        for c in range(2)
        for l in range(n_l)
        for y in range(2)
    ]


def split_columns(a, b, part, order, total):
    shape = jax.ShapeDtypeStruct((len(order), a.shape[0], total), a.dtype)
    return pl.pallas_call(
        functools.partial(split_kernel, part, order), out_shape=[shape] * 2, name="split_columns"
    )(a, b)


def join_columns(a, b, part, order):
    shape = jax.ShapeDtypeStruct((a.shape[1], len(order) * len(order[0]) * part), wide)
    return pl.pallas_call(
        functools.partial(join_kernel, part, order), out_shape=[shape] * 2, name="join_columns"
    )(a, b)


def first_allowed(ends_ref, count, places):
    start = jnp.zeros_like(places)
    for j in range(count):
        end = ends_ref[j]
        start = jnp.where(places >= end, end, start)
    return jnp.where(places >= ends_ref[count - 1], places, start)


def contract(left, right, dims):
    return lax.dot_general(left, right, (dims, ((), ())), preferred_element_type=wide)


def stacked(ref, span, heads, width):
    return jnp.concatenate(
        [ref[span, j * width : (j + 1) * width] for j in range(heads)], axis=0
    )


def tile_mask(ends_ref, begin, tile, length, heads):
    rows = begin + lax.broadcasted_iota(jnp.int32, (tile, 1), 0)
    lows = first_allowed(ends_ref, ends_ref.shape[0], rows)
    rows = jnp.concatenate([rows] * heads, axis=0)
    lows = jnp.concatenate([lows] * heads, axis=0)
    columns = lax.broadcasted_iota(jnp.int32, (heads * tile, length), 1)
    return (columns >= lows) & (columns <= rows)


def attend_kernel(heads, tile, ends_ref, q_ref, k_ref, v_ref, o_ref, log_ref):
    width = k_ref.shape[1]
    for i in range(q_ref.shape[0] // tile):
        span, length = slice(i * tile, (i + 1) * tile), (i + 1) * tile
        mask = tile_mask(ends_ref, i * tile, tile, length, heads)
        scores = contract(stacked(q_ref, span, heads, width), k_ref[:length, :], ((1,), (1,)))
        scores = jnp.where(mask, scores, masked_value)
        top = jnp.max(scores, axis=1, keepdims=True)
        weights = jnp.exp(scores - top)
        total = jnp.sum(weights, axis=1, keepdims=True)
        mixed = contract(weights.astype(low), v_ref[:length, :], ((1,), (0,))) / total
        log = jnp.broadcast_to(top + jnp.log(total), (heads * tile, 128))
        for j in range(heads):
            part = slice(j * tile, (j + 1) * tile)
            o_ref[span, j * width : (j + 1) * width] = mixed[part].astype(low)
            log_ref[j, span, :] = log[part]


def attend_back_kernel(
    heads, tile, scale, ends_ref, q_ref, g_ref, o_ref, k_ref, v_ref, log_ref, cos_ref, sin_ref,
    dq_ref, dkv_ref, sum_ref,
):
    width = k_ref.shape[1]
    half = width // 2
    sum_ref[...] = jnp.zeros_like(sum_ref)
    for i in range(q_ref.shape[0] // tile):
        span, length = slice(i * tile, (i + 1) * tile), (i + 1) * tile
        mask = tile_mask(ends_ref, i * tile, tile, length, heads)
        queries = stacked(q_ref, span, heads, width)
        grads = stacked(g_ref, span, heads, width)
        outs = stacked(o_ref, span, heads, width)
        delta = jnp.sum(grads.astype(wide) * outs.astype(wide), axis=1, keepdims=True)
        log = jnp.concatenate([log_ref[j, span, :1] for j in range(heads)], axis=0)
        keys, values = k_ref[:length, :], v_ref[:length, :]
        scores = contract(queries, keys, ((1,), (1,)))
        weights = jnp.where(mask, jnp.exp(scores - log), 0.0)
        dprob = contract(grads, values, ((1,), (1,)))
        dscore = (weights * (dprob - delta)).astype(low)
        sum_ref[:length, width:] += contract(weights.astype(low), grads, ((0,), (0,)))
        sum_ref[:length, :width] += contract(dscore, queries, ((0,), (0,)))
        dquery = contract(dscore, keys, ((1,), (0,))) * scale
        cosine, sine = cos_ref[span, :], sin_ref[span, :]
        for j in range(heads):
            a = dquery[j * tile : (j + 1) * tile, :half]
            b = dquery[j * tile : (j + 1) * tile, half:]
            at = j * width
            dq_ref[span, at : at + half] = (a * cosine + b * sine).astype(low)
            dq_ref[span, at + half : at + width] = (b * cosine - a * sine).astype(low)
    dkv_ref[...] = sum_ref[...].astype(low)


def attend_whole_kernel(
    heads, tile, scale, ends_ref, packed_ref, up_ref, cos_ref, sin_ref, own_ref, other_ref,
    q_ref, o_ref, log_ref, terms_ref, out_ref,
):
    x = lax.axis_index("x")
    width = up_ref.shape[1] // heads
    half, low_width = width // 2, up_ref.shape[0]
    rows = own_ref.shape[0]
    out_ref[pl.ds(pl.multiple_of(x * rows, rows), rows), :] = own_ref[...]
    out_ref[pl.ds(pl.multiple_of(other(x) * rows, rows), rows), :] = other_ref[...]
    for i in range(q_ref.shape[0] // tile):
        span, length = slice(i * tile, (i + 1) * tile), (i + 1) * tile
        raw = jnp.dot(packed_ref[span, :low_width], up_ref[...], preferred_element_type=wide)
        cosine, sine = cos_ref[span, :] * scale, sin_ref[span, :] * scale
        queries = []
        for j in range(heads):
            a, b = turn(raw[:, j * width : (j + 1) * width], cosine, sine)
            q_ref[span, j * width : j * width + half] = a.astype(low)
            q_ref[span, j * width + half : (j + 1) * width] = b.astype(low)
        mask = tile_mask(ends_ref, i * tile, tile, length, heads)
        keys = packed_ref[:length, low_width : low_width + width]
        values = packed_ref[:length, low_width + width :]
        scores = contract(stacked(q_ref, span, heads, width), keys, ((1,), (1,)))
        scores = jnp.where(mask, scores, masked_value)
        top = jnp.max(scores, axis=1, keepdims=True)
        weights = jnp.exp(scores - top)
        total = jnp.sum(weights, axis=1, keepdims=True)
        mixed = contract(weights.astype(low), values, ((1,), (0,))) / total
        log = jnp.broadcast_to(top + jnp.log(total), (heads * tile, 128))
        for j in range(heads):
            part = slice(j * tile, (j + 1) * tile)
            o_ref[span, j * width : (j + 1) * width] = mixed[part].astype(low)
            log_ref[j, span, :] = log[part]
        terms_ref[span, :] = jnp.dot(
            o_ref[span, :], out_ref[...], preferred_element_type=wide
        ).astype(low)


def attend_whole(ends, packed, up_query, cosine, sine, own_heads, other_heads, heads, scale):
    length, width = packed.shape[0], own_heads.shape[1]
    columns = up_query.shape[1]
    vmem = pl.BlockSpec(memory_space=pltpu.VMEM)
    return pl.pallas_call(
        functools.partial(attend_whole_kernel, heads, tile_of(length), scale),
        in_specs=[pl.BlockSpec(memory_space=pltpu.SMEM)] + [vmem] * 6,
        out_specs=[vmem] * 5,
        out_shape=[
            jax.ShapeDtypeStruct((length, columns), low),
            jax.ShapeDtypeStruct((length, columns), low),
            jax.ShapeDtypeStruct((heads, length, 128), wide),
            jax.ShapeDtypeStruct((length, width), low),
            jax.ShapeDtypeStruct((columns, width), low),
        ],
        compiler_params=pltpu.CompilerParams(vmem_limit_bytes=56 * 1024 * 1024),
        cost_estimate=pl.CostEstimate(
            flops=12 * length * length * columns,
            bytes_accessed=16 * length * columns,
            transcendentals=length * length * heads // 2,
        ),
        name="attend",
    )(ends, packed, up_query, cosine, sine, own_heads, other_heads)


def tile_of(length):
    return next(t for t in (256, 128, 64, 32, 16, 8) if length % t == 0)


def attend(ends, query, packed, heads):
    length, width = query.shape[0], query.shape[1] // heads
    tile = tile_of(length)
    first = packed.shape[1] // width - 2
    return pl.pallas_call(
        functools.partial(attend_kernel, heads, tile),
        grid=(1,),
        in_specs=[
            pl.BlockSpec(memory_space=pltpu.SMEM),
            pl.BlockSpec((length, heads * width), lambda i: (0, 0)),
            pl.BlockSpec((length, width), lambda i: (0, first)),
            pl.BlockSpec((length, width), lambda i: (0, first + 1)),
        ],
        out_specs=[
            pl.BlockSpec((length, heads * width), lambda i: (0, 0)),
            pl.BlockSpec((heads, length, 128), lambda i: (0, 0, 0)),
        ],
        out_shape=[
            jax.ShapeDtypeStruct((length, heads * width), low),
            jax.ShapeDtypeStruct((heads, length, 128), wide),
        ],
        compiler_params=pltpu.CompilerParams(vmem_limit_bytes=56 * 1024 * 1024),
        cost_estimate=pl.CostEstimate(
            flops=6 * length * length * width * heads,
            bytes_accessed=8 * length * width * heads,
            transcendentals=length * length * heads // 2,
        ),
        name="attend",
    )(ends, query, packed, packed)


def attend_back(ends, query, grad, mixed, packed, logs, cosine, sine, heads, scale):
    length, width = query.shape[0], query.shape[1] // heads
    tile = tile_of(length)
    first = packed.shape[1] // width - 2
    rows = pl.BlockSpec((length, heads * width), lambda i: (0, 0))
    angle = pl.BlockSpec((length, width // 2), lambda i: (0, 0))
    return pl.pallas_call(
        functools.partial(attend_back_kernel, heads, tile, scale),
        grid=(1,),
        in_specs=[
            pl.BlockSpec(memory_space=pltpu.SMEM),
            rows,
            rows,
            rows,
            pl.BlockSpec((length, width), lambda i: (0, first)),
            pl.BlockSpec((length, width), lambda i: (0, first + 1)),
            pl.BlockSpec((heads, length, 128), lambda i: (0, 0, 0)),
            angle,
            angle,
        ],
        out_specs=[rows, pl.BlockSpec((length, 2 * width), lambda i: (0, 0))],
        out_shape=[
            jax.ShapeDtypeStruct((length, heads * width), low),
            jax.ShapeDtypeStruct((length, 2 * width), low),
        ],
        scratch_shapes=[pltpu.VMEM((length, 2 * width), wide)],
        compiler_params=pltpu.CompilerParams(vmem_limit_bytes=56 * 1024 * 1024),
        cost_estimate=pl.CostEstimate(
            flops=10 * length * length * width * heads,
            bytes_accessed=16 * length * width * heads,
            transcendentals=length * length * heads // 2,
        ),
        name="attend_back",
    )(ends, query, grad, mixed, packed, packed, logs, cosine, sine)


def on_device(
    tokens,
    lengths,
    cotangent,
    norm_one,
    query_down,
    query_gain,
    query_up,
    key_proj,
    value_proj,
    out_proj,
    norm_two,
    gate_proj,
    up_proj,
    down_proj,
):
    n_x, n_l = lax.axis_size("x"), lax.axis_size("l")
    x, c, h, l, y = [lax.axis_index(a) for a in every]
    n_dev = n_x * 8 * n_l
    n_group = 4 * n_l
    me = group_place()
    count, width = tokens.shape
    row_len = count * n_group
    latent_width = query_down.shape[1]
    head_dim = key_proj.shape[1]
    shard = query_down.shape[0]
    heads = query_up.shape[1] // head_dim // n_group
    ff_part = down_proj.shape[0]
    ff_own = ff_part * n_x * 2
    ff_pad = -(-ff_own // 128) * 128
    natural = n_x == 2 and n_l == 2
    scale = 1.0 / math.sqrt(head_dim)
    order = column_order(n_x, n_l)
    mapped_width = latent_width + 2 * head_dim

    gains = jnp.zeros((shard, 128), low)
    gains = gains.at[0, :shard].set(norm_one).at[1, :shard].set(norm_two)
    gains = gains.at[2, : query_gain.shape[0]].set(query_gain)
    small = jnp.concatenate([query_down, key_proj, value_proj, gains], axis=1)
    rows_up = query_up.shape[0]
    if natural:
        head_cols = query_up.reshape(rows_up, 2, 2, 2, 2, head_dim)
        head_cols = head_cols.transpose(2, 4, 3, 0, 1, 5)
    else:
        head_cols = query_up.reshape(rows_up, n_group, -1).transpose(1, 0, 2)
    head_cols = head_cols.reshape(n_group, rows_up, heads * head_dim)
    if natural:
        lens = jnp.pad(lengths, ((0, 7), (0, 128 - lengths.shape[1])))
        in_full, own_heads, (up_query, gate_rows, up_rows), (home, lens) = open_exchange(
            small, out_proj, head_cols, gate_proj, up_proj, [tokens, lens], ff_part, order, ff_pad
        )
        row_lengths = lens[0, : lengths.shape[1]]
    else:
        in_full = lax.all_gather(small, every, axis=0)
        home, grad_home, row_lengths = [swap_home(a) for a in (tokens, cotangent, lengths)]
        row_lengths = row_lengths[0]
        gate_cols, up_cols = split_columns(gate_proj, up_proj, ff_part, order, ff_pad)
        up_query, gate_rows, up_rows = [
            all_to_all_row(a) for a in (head_cols, gate_cols, up_cols)
        ]
        up_query = up_query.reshape((2, -1) + up_query.shape[1:])
        up_query = lax.all_gather(lax.all_gather(up_query, "h", axis=1), "x", axis=0)
    up_query = up_query.reshape(latent_width, -1)
    gate_rows = gate_rows.reshape(2, -1, ff_pad)
    up_rows = up_rows.reshape(2, -1, ff_pad)
    gain_one = in_full[:, 0, mapped_width : mapped_width + shard].reshape(width).astype(wide)
    gain_two = in_full[:, 1, mapped_width : mapped_width + shard].reshape(width).astype(wide)
    gain_latent = in_full[:, 2, mapped_width : mapped_width + query_gain.shape[0]]
    gain_latent = gain_latent.reshape(latent_width).astype(wide)
    in_full = in_full.reshape(width, -1)

    inputs = home.astype(wide)
    mapped_rates = jnp.exp(
        jnp.arange(head_dim // 2, dtype=wide) * (-math.log(10000.0) / (head_dim // 2))
    )
    ends = jnp.cumsum(row_lengths, dtype=jnp.int32)
    places = jnp.arange(row_len, dtype=jnp.int32)
    begins = jnp.max(jnp.where(places[:, None] >= ends[None, :], ends[None, :], 0), axis=1)
    if not natural:
        phases = (places - begins).astype(wide)[:, None] * mapped_rates
        cosine, sine = jnp.cos(phases), jnp.sin(phases)
        own_cos = lax.dynamic_slice_in_dim(cosine, me * count, count)
        own_sin = lax.dynamic_slice_in_dim(sine, me * count, count)

    if natural:
        own_heads = own_heads.reshape(-1, width)
        gate_a, gate_b, up_a, up_b = gate_rows[0], gate_rows[1], up_rows[0], up_rows[1]
        down_a, down_b = down_proj[:, : width // 2], down_proj[:, width // 2 :]
        heads_x = flip(own_heads, "x")
    else:
        out_full = lax.all_gather(out_proj, every, axis=0, tiled=True)
        out_own = lax.dynamic_slice_in_dim(out_full, me * heads * head_dim, heads * head_dim)
        gate_own, up_own = [
            lax.all_gather(lax.all_gather(a, "h", axis=1), "x", axis=0).reshape(width, -1)
            for a in (gate_rows, up_rows)
        ]
        down_own = lax.all_gather(lax.all_gather(down_proj, "h", axis=0), "x", axis=0)
        down_own = jnp.pad(down_own.reshape(-1, width), ((0, ff_pad - ff_own), (0, 0)))

    scale_one = rms_scale(inputs)
    if natural:
        packed, hidden, latent, cosine, sine, gate_a_h, gate_b_h = front(
            ends, home, in_full, gain_one[None], gain_latent[None], mapped_rates[None], row_len, 2,
            ("h", "h"), (gate_a, gate_b),
        )
        own_cos = lax.dynamic_slice_in_dim(cosine, me * count, count)
        own_sin = lax.dynamic_slice_in_dim(sine, me * count, count)
        packed, heads_x, up_a = together(packed, heads_x, up_a)
        up_a_h, up_b_h = flip(up_a, "h"), flip(after(up_b, packed), "h")
        gate_x = [flip(a, "x") for a in (gate_a, gate_b, gate_a_h, gate_b_h)]
        all_latent = packed[:, :latent_width]
        query, mixed, logs, terms, out_own = attend_whole(
            ends, packed, up_query, cosine, sine, own_heads, heads_x, heads, scale
        )
        terms, up_a_h, up_b_h = together(terms, up_a_h, up_b_h)
        up_x = [flip(a, "x") for a in (up_a, up_b, up_a_h, up_b_h)]
        attended, down_a_h, down_b_h = scatter_row(3, terms, kinds=("h", "h"), more=(down_a, down_b))
        attended, gate_x, up_x = together(attended, gate_x, up_x)
    else:
        hidden = (inputs * scale_one * gain_one).astype(low)
        mapped = dot(hidden, in_full)
        latent = mapped[:, :latent_width]
        scale_latent = rms_scale(latent)
        latent_low = (latent * scale_latent * gain_latent).astype(low)
        keys = mapped[:, latent_width : latent_width + head_dim]
        keys = rotate(keys, own_cos, own_sin).astype(low)
        values = mapped[:, latent_width + head_dim : mapped_width].astype(low)
        packed = gather_row(jnp.concatenate([latent_low, keys, values], axis=1), 2)
        grad_all = lax.all_gather(grad_home, group, axis=0, tiled=True)
        all_latent = packed[:, :latent_width]
        query_raw = dot(all_latent, up_query)
        query = jnp.concatenate(
            [
                rotate(query_raw[:, j * head_dim : (j + 1) * head_dim], cosine, sine)
                for j in range(heads)
            ],
            axis=1,
        ).astype(low) * jnp.asarray(scale, low)
        mixed, logs = attend(ends, query, packed, heads)
        attended = scatter_row(3, dot(mixed, out_own, low))[0]
    resid = inputs + attended
    scale_two = rms_scale(resid)
    hidden_two = (resid * scale_two * gain_two).astype(low)
    if natural:
        gate_parts = [gate_a, gate_b, gate_a_h, gate_b_h] + list(gate_x)
        up_parts = [up_a, up_b, up_a_h, up_b_h] + list(up_x)
        (
            all_two, inner, gate_factor, up_factor, down_a_x, down_a_xh, down_b_x, down_b_xh,
            grad_home, grad_all,
        ) = feed_forward(
            hidden_two, gate_parts, up_parts, (down_a, down_a_h, down_b, down_b_h), cotangent, 4
        )
    else:
        all_two = gather_row(hidden_two, 4)
        gate = dot(all_two, gate_own)
        upward = dot(all_two, up_own)
        sigma = jax.nn.sigmoid(gate)
        inner = (gate * sigma * upward).astype(low)
        grad_down = outer_sum(inner, grad_all, low)

    if natural:
        (
            dhidden_two, *spread, gate_terms, gate_x, up_terms, up_x, grad_down, _, _
        ) = feed_back(
            grad_all,
            gate_factor,
            up_factor,
            inner,
            all_two,
            gate_parts,
            up_parts,
            [
                (down_a, down_a_h, down_a_x, down_a_xh),
                (down_b, down_b_h, down_b_x, down_b_xh),
            ],
            5,
        )
    else:
        dinner = times_transposed(grad_all, down_own)
        dgate = (dinner * upward * sigma * (1.0 + gate * (1.0 - sigma))).astype(low)
        dupward = (dinner * gate * sigma).astype(low)
        grad_gate, grad_upward = outer_sum(all_two, dgate, low), outer_sum(all_two, dupward, low)
        dhidden_two = times_transposed(dgate, gate_own) + times_transposed(dupward, up_own)
        dhidden_two = scatter_row(5, dhidden_two.astype(low))[0]
        spread = scatter_row(6, dot(inner, down_own, low))[0]
        grad_down = sum_columns(grad_down[:ff_own].reshape(n_x, 2, ff_part, width), 0).astype(wide)
        gate_terms, up_terms = [
            sum_columns(a.reshape(n_x, 2, 2, -1, ff_pad), 1) for a in (grad_gate, grad_upward)
        ]

    dresid_part, dgain_two = norm_back(dhidden_two, resid, scale_two, gain_two)
    dresid = grad_home.astype(wide) + dresid_part
    branch = dresid.astype(low)
    if natural:
        by_h = (2, 2, -1, ff_pad)
        dlow, dkv, gate_terms, up_terms, final, out_terms, head_terms, *_ = middle(
            ends, branch, (gate_terms.reshape(by_h), gate_x.reshape(by_h)),
            (up_terms.reshape(by_h), up_x.reshape(by_h)), spread, query, mixed, packed, logs, cosine,
            sine, out_own, up_query, resid, heads, scale, 7,
        )
        gate_terms, up_terms = [a.reshape(n_group, shard, ff_pad) for a in (gate_terms, up_terms)]
        head_terms = head_terms.reshape(n_group, rows_up, heads * head_dim)
        summed, grad_tokens, output, grad_gate, grad_upward, grad_uquery, grad_out = shut(
            dlow, dkv, latent, gain_latent[None], own_cos, own_sin, hidden,
            in_full.reshape(n_dev, shard, -1), home, gain_one[None], dresid, dgain_two[None],
            gate_terms, up_terms, head_terms, final, pick(out_terms, h), pick(out_terms, 1 - h),
            ff_part, order, 9,
        )
    else:
        branch_all = gather_row(branch, 7)
        grad_out = outer_sum(mixed, branch_all, low)
        dmixed = times_transposed(branch_all, out_own, low)
        dquery, dkv = attend_back(
            ends, query, dmixed, mixed, packed, logs, cosine, sine, heads, scale
        )
        dlow = times_transposed(dquery, up_query, low)
        head_terms = outer_sum(all_latent, dquery, low).reshape(n_x, 2, 2, -1, heads * head_dim)
        dlow, dkv = scatter_row(8, dlow, dkv)
        whole = jnp.zeros((n_group * heads * head_dim, width), wide)
        whole = lax.dynamic_update_slice_in_dim(
            whole, grad_out.astype(wide), me * heads * head_dim, 0
        )
        grad_out = lax.psum_scatter(whole, every, scatter_dimension=0, tiled=True)
        final = (resid + spread).astype(low)
        dkeys = rotate_back(dkv[:, :head_dim], own_cos, own_sin).astype(low)
        dvalues = dkv[:, head_dim:].astype(low)
        dlatent, dgain_latent = norm_back(dlow, latent, scale_latent, gain_latent)
        nothing = jnp.zeros((count, 128), low)
        dmapped = jnp.concatenate([dlatent.astype(low), dkeys, dvalues, nothing], axis=1)
        dhidden = times_transposed(dmapped, in_full)
        dinput_part, dgain_one = norm_back(dhidden, inputs, scale_one, gain_one)
        grad_tokens = (dresid + dinput_part).astype(low)
        grad_in = outer_sum(hidden, dmapped[:, :mapped_width], low).reshape(n_dev, shard, -1)
        gain_terms = jnp.zeros((n_dev, shard, 128), low)
        gain_terms = gain_terms.at[:, 0, :shard].set(dgain_one.reshape(n_dev, -1).astype(low))
        gain_terms = gain_terms.at[:, 1, :shard].set(dgain_two.reshape(n_dev, -1).astype(low))
        gain_terms = gain_terms.at[:, 2, : query_gain.shape[0]].set(
            dgain_latent.reshape(n_dev, -1).astype(low)
        )
        terms = jnp.concatenate([grad_in, gain_terms], axis=2)
        summed = lax.psum_scatter(terms.astype(wide), every, scatter_dimension=0, tiled=False)
        grad_tokens, output = swap_home(grad_tokens), swap_home(final)
        head_terms = all_to_all_row(
            sum_columns(head_terms, 1).reshape(n_group, rows_up, heads * head_dim)
        )
        gate_terms, up_terms = [
            all_to_all_row(a.reshape(n_group, shard, ff_pad)) for a in (gate_terms, up_terms)
        ]
        grad_gate, grad_upward = join_columns(gate_terms, up_terms, ff_part, order)
        grad_uquery = head_terms.transpose(1, 0, 2).reshape(rows_up, -1).astype(wide)
    return (
        output,
        grad_tokens.astype(wide),
        summed[0, mapped_width : mapped_width + shard],
        summed[:, :latent_width],
        summed[2, mapped_width : mapped_width + query_gain.shape[0]],
        grad_uquery,
        summed[:, latent_width : latent_width + head_dim],
        summed[:, latent_width + head_dim : mapped_width],
        grad_out,
        summed[1, mapped_width : mapped_width + shard],
        grad_gate,
        grad_upward,
        grad_down,
    )


def solution(mesh):
    n_dp, n_seq = mesh.shape["dp"], mesh.shape["seq"]
    fine = Mesh(mesh.devices.reshape(n_dp // 2, 2, 2, n_seq // 4, 2), every)
    rows, flat = P(every, None), P(every)
    placed = (rows, P(("x", "c"), None), rows, flat, rows, flat) + (rows,) * 4 + (flat,) + (rows,) * 3
    return jax.shard_map(
        on_device,
        mesh=fine,
        in_specs=placed,
        out_specs=(rows, rows, flat, rows, flat) + (rows,) * 4 + (flat,) + (rows,) * 3,
        check_vma=False,
    )
```

profile of v0, /device:TPU:0, one launch (start us, length us, event | category | flops | bytes accessed | tf_op | source)
XLA Modules:
  0.0 585.0 jit_solution(17838809891704335263)
XLA Ops:
  0.7 1.2 reshape.255
  2.0 0.2 copy.29
  2.2 0.2 reshape.256.heads_in
  2.4 0.2 scatter.11
  2.6 0.2 scatter.14
  2.8 1.1 copy-done.10
  4.0 1.1 copy-done.11
  5.1 1.1 copy-done.12
  6.2 66.4 %open_exchange.1 = (bf16[32,64,1664]{2,1,0:T(8,128)(2,1)S(1)}, bf16[2,128,2048]{2,1,0:T(8,128)(2,1)}, bf16[2,2,2,4,32,512]{5,4,3,2,1,0:T(8,128)(2,1)S(1)}, bf16[...) custom-call(bf16[64,1664]{1,0:T(8,128)(2,1)S(1)} %pad_maximum_fusion, ...), custom_call_target="tpu_custom_call" | custom-call | bytes 157286400 | tf_op jit(solution)/shard_map/open_exchange/pallas_call | solution.py:360
  72.6 1.0 copy-done.20
  73.6 1.0 collective-permute-start
  74.7 1.1 collective-permute-start.3
  75.7 0.9 copy-done
  76.6 0.1 convert_reduce_fusion
  76.7 0.1 reshape.271.gain_ref.refs_9_
  76.8 0.9 convert_reduce_fusion.1
  77.7 0.1 reshape.272.low_gain_ref.refs_3_
  77.7 0.2 reduce-window.9
  78.0 2.9 copy-done.1
  80.9 48.5 %front.1 = (bf16[8,192,1536]{2,1,0:T(8,128)(2,1)S(1)}, bf16[192,2048]{1,0:T(8,128)(2,1)S(1)}, f32[192,1024]{1,0:T(8,128)S(1)}, f32[1536,128]{1,0:T(8,128)S(1)}, ...) custom-call(s32[8]{0:T(128)S(1)} %bitcast.46, ...), custom_call_target="tpu_custom_call" | custom-call | bytes 104857600 | tf_op jit(solution)/shard_map/front/pallas_call | solution.py:470
  129.4 0.9 copy-done.8
  130.3 0.9 copy-done.17
  131.2 2.1 copy-done.19
  133.4 2.0 collective-permute-start.6
  135.6 0.1 collective-permute-start.2
  135.6 2.9 collective-permute-start.1
  138.6 22.5 %attend.1 = (bf16[1536,512]{1,0:T(8,128)(2,1)}, bf16[1536,512]{1,0:T(8,128)(2,1)}, f32[2,1536,128]{2,1,0:T(8,128)}, bf16[1536,2048]{1,0:T(8,128)(2,1)}, bf16[512,2048]{1,0:T(8,128)(2,1)}) custom-call(s32[8]{0:T(128)} %bitcast.47, bf16[1536,1536]{1,0:T(8,128)(2,1)} %bitcast.49, bf16[1024,512]{1,0:T(8,128)(2,1)} %bitcast.51, f32[1536,128]{1,0:T(8,128)} %copy-done.16, ...), custom_call_target="tpu_custom_call" | custom-call | flops 14495514624 | bytes 12582912 | tf_op jit(solution)/shard_map/attend/pallas_call | solution.py:2026
  161.1 1.1 collective-permute-done.2.refs_12_.refs_16_
  162.1 0.9 collective-permute-start.4
  163.0 7.4 %collective-permute-done.1.refs_11_.refs_15_ = bf16[256,768]{1,0:T(8,128)(2,1)} collective-permute-done((bf16[256,768]{1,0:T(8,128)(2,1)S(1)}, bf16[256,768]{1,0:T(8,128)(2,1)}, u32[]{:S(2)}, u32[]{:S(2)}) %collective-permute-start.1) | collective-permute-done | bytes 393248 | tf_op jit(solution)/shard_map/ppermute | solution.py:72
  170.5 0.9 collective-permute-start.8
  171.4 1.2 collective-permute-start.7
  172.6 0.9 collective-permute-start.10
  173.5 1.2 collective-permute-start.9
  174.7 1.6 constant_dynamic-slice_fusion
  176.5 3.0 copy-done.3
  179.5 39.8 %scatter_row.1 = (f32[192,2048]{1,0:T(8,128)S(1)}, bf16[176,1024]{1,0:T(8,128)(2,1)S(1)}, bf16[176,1024]{1,0:T(8,128)(2,1)S(1)}) custom-call(bf16[8,192,2048]{2,1,0:T(8,128)(2,1)S(1)} %bitcast.37, bf16[176,1024]{1,0:T(8,128)(2,1)S(1)} %get-tuple-element.204.refs_1_.refs_17_.refs_21_, bf16[176,1024]{1,0:T(8,128)(2,1)S(1)} %get-tuple-element.203.refs_2_.refs_19_.refs_25_), custom_call_target="tpu_custom_call" | custom-call | bytes 83886080 | tf_op jit(solution)/shard_map/scatter_row/pallas_call | solution.py:1187
  219.4 0.3 multiply_reduce_fusion.2
  219.7 0.4 copy-done.23
  220.1 0.1 copy-done.24
  220.2 0.1 copy-done.48
  220.4 1.1 copy-done.25
  221.5 1.1 multiply_convert_fusion.refs_0_
  222.6 67.1 %feed_forward.1 = (bf16[8,192,2048]{2,1,0:T(8,128)(2,1)}, bf16[8,192,768]{2,1,0:T(8,128)(2,1)}, bf16[8,192,768]{2,1,0:T(8,128)(2,1)}, bf16[8,192,768]{2,1,0:T(8,...) custom-call(bf16[192,2048]{1,0:T(8,128)(2,1)} %multiply_convert_fusi, ...), custom_call_target="tpu_custom_call" | custom-call | flops 9663676416 | bytes 104857600 | tf_op jit(solution)/shard_map/feed_forward/pallas_call | solution.py:801
  289.7 68.0 %feed_back.1 = (f32[192,2048]{1,0:T(8,128)}, bf16[4,192,2048]{2,1,0:T(8,128)(2,1)}, bf16[4,192,2048]{2,1,0:T(8,128)(2,1)}, bf16[1024,768]{1,0:T(8,128)(2,1)}, bf...) custom-call(bf16[8,192,2048]{2,1,0:T(8,128)(2,1)} %get-tuple-element, ...), custom_call_target="tpu_custom_call" | custom-call | flops 28991029248 | bytes 104857600 | tf_op jit(solution)/shard_map/feed_back/pallas_call | solution.py:1051
  357.8 2.6 multiply_reduce_fusion
  360.3 1.9 fusion
  362.3 126.6 %middle.1 = (f32[192,1024]{1,0:T(8,128)}, f32[192,512]{1,0:T(8,128)}, bf16[2,256,768]{2,1,0:T(8,128)(2,1)}, bf16[2,256,768]{2,1,0:T(8,128)(2,1)}, bf16[192,2048]...) custom-call(s32[8]{0:T(128)} %bitcast.48, ...), custom_call_target="tpu_custom_call" | custom-call | flops 21743271936 | bytes 209715200 | tf_op jit(solution)/shard_map/middle/pallas_call | solution.py:1553
  488.9 2.3 dynamic-slice_bitcast_fusion
  491.2 77.7 %shut.1 = (f32[64,1664]{1,0:T(8,128)}, f32[192,2048]{1,0:T(8,128)}, bf16[192,2048]{1,0:T(8,128)(2,1)}, f32[64,5632]{1,0:T(8,128)}, f32[64,5632]{1,0:T(8,128)}, /*index=5*/f32[32,4096]{1,0:T(8,128)}, f32[128,2048]{1,0:T(8,128)}) custom-call(f32[192,1024]{1,0:T(8,128)} %get-tuple-element.172.refs_0_, f32[192,512]{1,0:T(8,128)} %get-tuple-element.173.refs_1_, ...), custom_call_target="tpu_custom_call" | custom-call | bytes 157286400 | tf_op jit(solution)/shard_map/shut/pallas_call | solution.py:1823
  568.8 1.8 slice.117
  570.6 1.5 fusion.4
  572.2 1.3 slice_bitcast_fusion
  573.4 1.2 slice_bitcast_fusion.1
  574.6 2.1 copy.39
  576.7 1.1 copy.40
  577.9 0.2 copy-done.35
  578.1 0.8 copy.41
  578.9 1.0 copy.42
  579.9 1.1 copy.43
  581.0 0.8 copy-done.30
  581.7 1.1 copy.44
  582.8 0.8 copy-done.29
  583.6 1.1 copy.45
  (102 shorter events, 0.5 us)
Async XLA Ops:
  0.6 1.7 copy-start.41
  0.7 1.7 copy-start.42
  0.7 1.7 copy-start.43
  0.7 1.9 copy-start.44
  0.7 2.1 copy-start.38
  0.7 2.1 copy-start.40
  0.7 2.1 copy-start.39
  0.7 2.1 copy-start.13
  2.8 1.1 copy-start.10
  4.0 1.1 copy-start.11
  5.1 1.1 copy-start.12
  72.6 1.0 copy-start.20
  73.5 3.0 copy-start
  73.5 145.9 %copy-start.2 = (bf16[192,2048]{1,0:T(8,128)(2,1)}, bf16[192,2048]{1,0:T(8,128)(2,1)S(1)}, u32[]{:S(2)}) copy-start(bf16[192,2048]{1,0:T(8,128)(2,1)S(1)} %get-tuple-element.120.home_ref.refs_8_) | copy-start | bytes 2359300
  73.6 62.0 %collective-permute-start = (bf16[256,2048]{1,0:T(8,128)(2,1)}, bf16[256,2048]{1,0:T(8,128)(2,1)}, u32[]{:S(2)}, u32[]{:S(2)}) collective-permute-start(bf16[256,2048]{1,0:T(8,128)(2,1)} %bitcast.10.own_ref), channel_id=1, source_target_pairs={{0,16},{16,0},{1,17},{17,1},{2,18},{18,2},{3,19},{19,3},{4,20},{20... | collective-permute-start | bytes 3145736 | tf_op jit(solution)/shard_map/ppermute | solution.py:72
  74.6 54.7 %copy-start.5 = (bf16[4,64,768]{2,1,0:T(8,128)(2,1)}, bf16[4,64,768]{2,1,0:T(8,128)(2,1)S(1)}, u32[]{:S(2)}) copy-start(bf16[4,64,768]{2,1,0:T(8,128)(2,1)S(1)} %get-tuple-element.202) | copy-start | bytes 1179652
  74.7 87.5 %copy-start.4 = (bf16[4,64,768]{2,1,0:T(8,128)(2,1)}, bf16[4,64,768]{2,1,0:T(8,128)(2,1)S(1)}, u32[]{:S(2)}) copy-start(bf16[4,64,768]{2,1,0:T(8,128)(2,1)S(1)} %get-tuple-element.201) | copy-start | bytes 1179652
  74.7 98.8 %collective-permute-start.3 = (bf16[256,768]{1,0:T(8,128)(2,1)S(1)}, bf16[256,768]{1,0:T(8,128)(2,1)S(1)}, u32[]{:S(2)}, u32[]{:S(2)}) collective-permute-start(bf16[256,768]{1,0:T(8,128)(2,1)S(1)} %bitcast.42), channel_id=1, source_target_pairs={{0,16},{16,0},{1,17},{17,1},{2,18},{18,2},{3,19},{19,3},{4,20},{20... | collective-permute-start | bytes 1179656 | tf_op jit(solution)/shard_map/ppermute | solution.py:72
  76.8 52.6 %copy-start.14 = (f32[1,2048]{1,0:T(1,128)}, f32[1,2048]{1,0:T(1,128)S(1)}, u32[]{:S(2)}) copy-start(f32[1,2048]{1,0:T(1,128)S(1)} %reshape.271.gain_ref.refs_9_) | copy-start | bytes 24580
  77.7 51.6 %copy-start.15 = (f32[1,1024]{1,0:T(1,128)}, f32[1,1024]{1,0:T(1,128)S(1)}, u32[]{:S(2)}) copy-start(f32[1,1024]{1,0:T(1,128)S(1)} %reshape.272.low_gain_ref.refs_3_) | copy-start | bytes 12292
  77.9 51.5 %copy-start.18 = (s32[8,1]{0,1:T(1,128)}, s32[8,1]{0,1:T(1,128)S(1)}, u32[]{:S(2)}) copy-start(s32[8,1]{0,1:T(1,128)S(1)} %reduce-window.9) | copy-start | bytes 100
  77.9 2.9 copy-start.1
  129.4 0.9 copy-start.8
  130.3 0.9 copy-start.17
  131.2 2.1 copy-start.19
  133.3 2.2 copy-start.16
  133.3 27.7 %copy-start.9 = (f32[192,1024]{1,0:T(8,128)}, f32[192,1024]{1,0:T(8,128)S(1)}, u32[]{:S(2)}) copy-start(f32[192,1024]{1,0:T(8,128)S(1)} %get-tuple-element.174.refs_2_) | copy-start | bytes 2359300
  133.3 27.7 %copy-start.21 = (bf16[256,768]{1,0:T(8,128)(2,1)}, bf16[256,768]{1,0:T(8,128)(2,1)S(1)}, u32[]{:S(2)}) copy-start(bf16[256,768]{1,0:T(8,128)(2,1)S(1)} %get-tuple-element.136.refs_3_.refs_7_) | copy-start | bytes 1179652
  133.4 27.7 %copy-start.22 = (bf16[256,768]{1,0:T(8,128)(2,1)}, bf16[256,768]{1,0:T(8,128)(2,1)S(1)}, u32[]{:S(2)}) copy-start(bf16[256,768]{1,0:T(8,128)(2,1)S(1)} %get-tuple-element.137.refs_4_.refs_8_) | copy-start | bytes 1179652
  133.4 38.0 %collective-permute-start.5 = (bf16[256,768]{1,0:T(8,128)(2,1)S(1)}, bf16[256,768]{1,0:T(8,128)(2,1)S(1)}, u32[]{:S(2)}, u32[]{:S(2)}) collective-permute-start(bf16[256,768]{1,0:T(8,128)(2,1)S(1)} %get-tuple-element.136.refs_3_.refs_7_), channel_id=1, source_target_pairs={{0,16},{16,0},{1,17},{17,1},{2,18},{18,2},{3,19},{19,3},{4,20},{20... | collective-permute-start | bytes 1179656 | tf_op jit(solution)/shard_map/ppermute | solution.py:72
  133.4 39.1 %collective-permute-start.6 = (bf16[256,768]{1,0:T(8,128)(2,1)S(1)}, bf16[256,768]{1,0:T(8,128)(2,1)S(1)}, u32[]{:S(2)}, u32[]{:S(2)}) collective-permute-start(bf16[256,768]{1,0:T(8,128)(2,1)S(1)} %get-tuple-element.137.refs_4_.refs_8_), channel_id=1, source_target_pairs={{0,16},{16,0},{1,17},{17,1},{2,18},{18,2},{3,19},{19,3},{4,20},{20... | collective-permute-start | bytes 1179656 | tf_op jit(solution)/shard_map/ppermute | solution.py:72
  135.5 34.9 %copy-start.36 = (bf16[4,64,768]{2,1,0:T(8,128)(2,1)}, bf16[4,64,768]{2,1,0:T(8,128)(2,1)S(1)}, u32[]{:S(2)}) copy-start(bf16[4,64,768]{2,1,0:T(8,128)(2,1)S(1)} %get-tuple-element.199) | copy-start | bytes 1179652
  135.5 35.8 %copy-start.37 = (bf16[4,64,768]{2,1,0:T(8,128)(2,1)}, bf16[4,64,768]{2,1,0:T(8,128)(2,1)S(1)}, u32[]{:S(2)}) copy-start(bf16[4,64,768]{2,1,0:T(8,128)(2,1)S(1)} %get-tuple-element.200) | copy-start | bytes 1179652
  135.6 26.6 %collective-permute-start.2 = (bf16[256,768]{1,0:T(8,128)(2,1)S(1)}, bf16[256,768]{1,0:T(8,128)(2,1)}, u32[]{:S(2)}, u32[]{:S(2)}) collective-permute-start(bf16[256,768]{1,0:T(8,128)(2,1)S(1)} %bitcast.56), channel_id=1, source_target_pairs={{0,4},{4,0},{1,5},{5,1},{2,6},{6,2},{3,7},{7,3},{8,12},{12,8},{9,1... | collective-permute-start | bytes 1179656 | tf_op jit(solution)/shard_map/ppermute | solution.py:72
  135.6 34.8 %collective-permute-start.1 = (bf16[256,768]{1,0:T(8,128)(2,1)S(1)}, bf16[256,768]{1,0:T(8,128)(2,1)}, u32[]{:S(2)}, u32[]{:S(2)}) collective-permute-start(bf16[256,768]{1,0:T(8,128)(2,1)S(1)} %bitcast.60), channel_id=1, source_target_pairs={{0,4},{4,0},{1,5},{5,1},{2,6},{6,2},{3,7},{7,3},{8,12},{12,8},{9,1... | collective-permute-start | bytes 1179656 | tf_op jit(solution)/shard_map/ppermute | solution.py:72
  138.6 37.8 %copy-start.34 = (bf16[176,2048]{1,0:T(8,128)(2,1)S(1)}, bf16[176,2048]{1,0:T(8,128)(2,1)}, u32[]{:S(2)}) copy-start(bf16[176,2048]{1,0:T(8,128)(2,1)} %param.33) | copy-start | bytes 2162692
  162.1 57.2 %collective-permute-start.4 = (bf16[256,768]{1,0:T(8,128)(2,1)S(1)}, bf16[256,768]{1,0:T(8,128)(2,1)}, u32[]{:S(2)}, u32[]{:S(2)}) collective-permute-start(bf16[256,768]{1,0:T(8,128)(2,1)S(1)} %bitcast.39), channel_id=1, source_target_pairs={{0,16},{16,0},{1,17},{17,1},{2,18},{18,2},{3,19},{19,3},{4,20},{20... | collective-permute-start | bytes 1179656 | tf_op jit(solution)/shard_map/ppermute | solution.py:72
  170.5 48.9 %collective-permute-start.8 = (bf16[256,768]{1,0:T(8,128)(2,1)S(1)}, bf16[256,768]{1,0:T(8,128)(2,1)}, u32[]{:S(2)}, u32[]{:S(2)}) collective-permute-start(bf16[256,768]{1,0:T(8,128)(2,1)S(1)} %bitcast.57), channel_id=1, source_target_pairs={{0,16},{16,0},{1,17},{17,1},{2,18},{18,2},{3,19},{19,3},{4,20},{20... | collective-permute-start | bytes 1179656 | tf_op jit(solution)/shard_map/ppermute | solution.py:72
  171.4 2.1 copy-start.46
  171.4 48.0 %collective-permute-start.7 = (bf16[256,768]{1,0:T(8,128)(2,1)S(1)}, bf16[256,768]{1,0:T(8,128)(2,1)}, u32[]{:S(2)}, u32[]{:S(2)}) collective-permute-start(bf16[256,768]{1,0:T(8,128)(2,1)S(1)} %bitcast.61), channel_id=1, source_target_pairs={{0,16},{16,0},{1,17},{17,1},{2,18},{18,2},{3,19},{19,3},{4,20},{20... | collective-permute-start | bytes 1179656 | tf_op jit(solution)/shard_map/ppermute | solution.py:72
  172.6 2.1 copy-start.47
  172.6 46.8 %collective-permute-start.10 = (bf16[256,768]{1,0:T(8,128)(2,1)}, bf16[256,768]{1,0:T(8,128)(2,1)}, u32[]{:S(2)}, u32[]{:S(2)}) collective-permute-start(bf16[256,768]{1,0:T(8,128)(2,1)} %collective-permute-done.2.refs_12_.refs_16_), channel_id=1, source_target_pairs={{0,16},{16,0},{1,17},{17,1},{2,18},{18,2},{3,19},{19,3},{4,20},{20... | collective-permute-start | bytes 1179656 | tf_op jit(solution)/shard_map/ppermute | solution.py:72
  173.5 45.8 %copy-start.45 = (bf16[256,768]{1,0:T(8,128)(2,1)}, bf16[256,768]{1,0:T(8,128)(2,1)S(1)}, u32[]{:S(2)}) copy-start(bf16[256,768]{1,0:T(8,128)(2,1)S(1)} %collective-permute-done.3.refs_5_.refs_9_) | copy-start | bytes 1179652
  173.5 45.9 %collective-permute-start.9 = (bf16[256,768]{1,0:T(8,128)(2,1)}, bf16[256,768]{1,0:T(8,128)(2,1)S(1)}, u32[]{:S(2)}, u32[]{:S(2)}) collective-permute-start(bf16[256,768]{1,0:T(8,128)(2,1)} %collective-permute-done.1.refs_11_.refs_15_), channel_id=1, source_target_pairs={{0,16},{16,0},{1,17},{17,1},{2,18},{18,2},{3,19},{19,3},{4,20},{20... | collective-permute-start | bytes 1179656 | tf_op jit(solution)/shard_map/ppermute | solution.py:72
  176.4 42.9 %copy-start.6 = (bf16[176,1024]{1,0:T(8,128)(2,1)}, bf16[176,1024]{1,0:T(8,128)(2,1)S(1)}, u32[]{:S(2)}) copy-start(bf16[176,1024]{1,0:T(8,128)(2,1)S(1)} %get-tuple-element.203.refs_2_.refs_19_.refs_25_) | copy-start | bytes 1081348
  176.4 42.9 %copy-start.7 = (bf16[176,1024]{1,0:T(8,128)(2,1)}, bf16[176,1024]{1,0:T(8,128)(2,1)S(1)}, u32[]{:S(2)}) copy-start(bf16[176,1024]{1,0:T(8,128)(2,1)S(1)} %get-tuple-element.204.refs_1_.refs_17_.refs_21_) | copy-start | bytes 1081348
  176.4 3.0 copy-start.3
  219.4 0.8 copy-start.23
  219.4 0.9 copy-start.24
  219.4 0.9 copy-start.48
  220.4 1.1 copy-start.25
  289.7 68.0 %copy-start.26 = (f32[192,2048]{1,0:T(8,128)S(1)}, f32[192,2048]{1,0:T(8,128)}, u32[]{:S(2)}) copy-start(f32[192,2048]{1,0:T(8,128)} %copy-done.25) | copy-start | bytes 4718596
  357.7 2.6 copy-start.27
  357.7 2.6 copy-start.33
  568.8 7.9 %copy-start.28 = (f32[192,2048]{1,0:T(8,128)S(1)}, f32[192,2048]{1,0:T(8,128)}, u32[]{:S(2)}) copy-start(f32[192,2048]{1,0:T(8,128)} %get-tuple-element.227) | copy-start | bytes 4718596
  576.7 1.4 copy-start.35
  576.7 2.2 copy-start.32
  578.1 1.8 copy-start.31
  579.8 1.9 copy-start.30
  581.7 1.9 copy-start.29
where the time goes:
time: 591 us; the launch traced here: 585 us
  Pallas kernels  517 us (87%)
  local copies, waits for them, and re-layouts  39 us (7%)
  starting transfers between devices  12.3 us (2%)
  waiting for transfers between devices  8.51 us (1%)
  other arithmetic  7.09 us (1%)
    pallas_call x1, Pallas kernels, middle(): pl.pallas_call(functools.partial(middle_kernel, heads, tile_of(length), s...  127 us
    pallas_call x1, Pallas kernels, shut(): pl.pallas_call(functools.partial(shut_kernel, part, head_dim, order, len(...  77.7 us
    pallas_call x1, Pallas kernels, feed_back(): pl.pallas_call(functools.partial(feed_back_kernel, True, chunks), in_spec...  68 us
    pallas_call x1, Pallas kernels, feed_forward(): pl.pallas_call(functools.partial(feed_kernel, False, chunks), in_specs=[i...  67.1 us
    pallas_call x1, Pallas kernels, open_exchange(): pl.pallas_call(functools.partial(open_kernel, n_swaps, part, order), in_s...  66.4 us
    pallas_call x1, Pallas kernels, front(): pl.pallas_call(functools.partial(front_kernel, kinds), in_specs=[pl.Block...  48.5 us
    pallas_call x1, Pallas kernels, scatter_row(): pl.pallas_call(functools.partial(scatter_kernel, even, chunks, n, kinds),...  39.8 us
    unnamed x105, local copies, waits for them, and re-layouts  27 us
  transfers between devices with their start and end apart: 11, of which 2 were waited for; matrix products, arithmetic and copies ran while one was open for 1% of the time, Pallas kernels for 19%

commit v1 on v0

--- a/solution.py
+++ b/solution.py
@@ -410,7 +410,7 @@
 def front_kernel(kinds, ends_ref, home_ref, full_ref, gain_ref, low_gain_ref, rates_ref, *refs):
     n = len(kinds)
     more, refs = refs[:n], refs[n:]
-    out_ref, hidden_ref, latent_ref, cos_ref, sin_ref, refs = *refs[:5], refs[5:]
+    out_ref, hidden_ref, latent_ref, cos_ref, sin_ref, own_cos, own_sin, refs = *refs[:7], refs[7:]
     more_out, refs = refs[:n], refs[n:]
     full, own, sends, recvs, load_sem, store_sem, more_sems = refs
     beside = Beside(kinds, more, more_out, more_sems)
@@ -426,6 +426,8 @@
     hidden = (values * rms_scale(values) * gain_ref[...]).astype(low)
     hidden_ref[...] = hidden
     cosine, sine = angles(ends_ref, rates_ref[...], flow.me * count, count)
+    own_cos[...] = cosine
+    own_sin[...] = sine
     load.wait()
     mapped = jnp.dot(hidden, full[...], preferred_element_type=wide)
     latent = mapped[:, :low_width]
@@ -471,13 +473,15 @@
         functools.partial(front_kernel, kinds),
         in_specs=[pl.BlockSpec(memory_space=pltpu.SMEM), vmem, in_hbm(), vmem, vmem, vmem]
         + [in_hbm()] * len(more),
-        out_specs=[in_hbm()] + [vmem] * 4 + [in_hbm()] * len(more),
+        out_specs=[in_hbm()] + [vmem] * 6 + [in_hbm()] * len(more),
         out_shape=[
             jax.ShapeDtypeStruct((8,) + packed, low),
             jax.ShapeDtypeStruct((count, width), low),
             jax.ShapeDtypeStruct((count, low_width), wide),
             jax.ShapeDtypeStruct((row_len, half), wide),
             jax.ShapeDtypeStruct((row_len, half), wide),
+            jax.ShapeDtypeStruct((count, half), wide),
+            jax.ShapeDtypeStruct((count, half), wide),
         ]
         + [jax.ShapeDtypeStruct(a.shape, low) for a in more],
         scratch_shapes=[
@@ -1258,7 +1262,7 @@
     ends_ref, branch_ref, gate_mine, gate_across, up_mine, up_across, terms_own, terms_twin = refs[:8]
     query_ref, mixed_ref, packed_ref, logs_ref, cos_in, sin_in, out_in, up_in = refs[8:16]
     resid_ref, refs = refs[16], refs[17:]
-    dlow_out, dkv_out, gate_out, up_out, final_ref, by_h_ref, head_out = refs[:7]
+    dlow_out, dkv_out, gate_out, up_out, home_ref, by_h_ref, head_out = refs[:7]
     land_gate, land_up, land_twin, refs = *refs[7:10], refs[10:]
     xs, kv, q, o, logs, cos_ref, sin_ref, out_own, up_query, dq, dlow, dkv_sum, dkv = refs[:13]
     refs = refs[13:]
@@ -1287,7 +1291,8 @@
     up = SumColumns(
         up_mine, up_across, land_up, up_out, up_own, column_stage, up_h, up_sems, local_sems.at[1]
     )
-    greet([near, side, twin, over_x, over_h])
+    core, cross = lax.axis_index("c"), {"c": other(c), "h": other(h)}
+    greet([near, side, twin, over_x, over_h, cross])
     flow.begin(None)
     sp_twin = remote(terms_twin, land_twin, sp_sems.at[0, 0], sp_sems.at[1, 0], twin)
     sp_twin.start()
@@ -1475,6 +1480,24 @@
         sc_arrived(a, 0, k)
         near_out[span, :] = (both(a, near_at, k, span) + far_in[span, :].astype(wide)).astype(low)
         sc_start(near_out.at[span], near_in.at[span], a, 2, k, near)
+    sp_arrived(2)
+    sp_arrived(3)
+    resid_load = pltpu.make_async_copy(resid_ref, stage_c, local_sems.at[2, 0])
+    resid_load.start()
+    resid_load.wait()
+    total = sp_pair(me) + sp_side_in[...].astype(wide) + sp_near_in[...].astype(wide)
+    sp_copies[1].wait_send()
+    sp_far[...] = (stage_c[...] + total).astype(low)
+    to_home = remote(sp_far, home_ref, sp_sems.at[0, 4], sp_sems.at[1, 4], cross)
+
+    @pl.when(core != h)
+    def _():
+        to_home.start()
+
+    @pl.when(core == h)
+    def _():
+        home_ref[...] = sp_far[...]
+
     out_x.wait_recv()
     total = go[x].astype(wide) + came_o[...].astype(wide)
     go[x] = total.astype(low)
@@ -1491,13 +1514,6 @@
         gh.at[x, :, other(h)], came_hh, chain_sems.at[0, 3], chain_sems.at[1, 3], over_h
     )
     head_h.start()
-    sp_arrived(2)
-    sp_arrived(3)
-    resid_load = pltpu.make_async_copy(resid_ref, stage_c, local_sems.at[2, 0])
-    resid_load.start()
-    resid_load.wait()
-    total = sp_pair(me) + sp_side_in[...].astype(wide) + sp_near_in[...].astype(wide)
-    final_ref[...] = (stage_c[...] + total).astype(low)
     gate.end()
     outs = (dlow_out, dkv_out)
     for a, k, span in sc_parts:
@@ -1513,8 +1529,12 @@
     head_h.wait_recv()
     head_out[...] = (gh[x, :, h].astype(wide) + came_hh[...].astype(wide)).astype(low)
     up.end()
-    for copy in sp_copies + sc_copies + [out_x, out_y, head_x, head_h]:
+    for copy in sp_copies[:1] + sp_copies[2:] + sc_copies + [out_x, out_y, head_x, head_h]:
         copy.wait_send()
+
+    @pl.when(core != h)
+    def _():
+        to_home.wait()
 
 
 def middle(
@@ -1590,7 +1610,7 @@
             sem((7, chunks)),
             sem((2, 7, chunks)),
             sem((2, 7, chunks)),
-            sem((2, 4)),
+            sem((2, 5)),
             sem((2, 8)),
             sem((2, 8)),
             sem((2, 4)),
@@ -1622,13 +1642,13 @@
     ins, outs, refs = refs[:n_in], refs[n_in : n_in + n_out], refs[n_in + n_out :]
     (
         dlow_ref, dkv_ref, latent_ref, gain_latent_ref, cos_ref, sin_ref, hidden_ref, in_full_ref,
-        home_ref, gain_one_ref, dresid_ref, gain_two_ref, gate_ref, up_ref, heads_ref, final_ref,
-        kept_ref, across_ref,
+        home_ref, gain_one_ref, dresid_ref, gain_two_ref, gate_ref, up_ref, heads_ref, kept_ref,
+        across_ref,
     ) = ins
-    sum_ref, tokens_ref, output_ref, gate_out, up_out, heads_out, out_ref = outs
+    sum_ref, tokens_ref, gate_out, up_out, heads_out, out_ref = outs
     full, mapped, terms, gains, twin_buf, held, came, moved, swap_buf = refs[:9]
-    gate_in, up_in, heads_in, final_buf, across_in = refs[9:14]
-    sends, recvs, set_sends, set_recvs, swap_sems, local_sems = refs[14:]
+    gate_in, up_in, heads_in, across_in = refs[9:13]
+    sends, recvs, set_sends, set_recvs, swap_sems, local_sems = refs[13:]
     x, c, h, l, y = [lax.axis_index(a) for a in every]
     hops = {
         1: {"h": other(h)},
@@ -1674,19 +1694,7 @@
     for copy in set_loads:
         copy.start()
     exchange = remote(across_ref, across_in, swap_sems.at[0], swap_sems.at[1], hops[1])
-    output_move = remote(final_ref, output_ref, swap_sems.at[2], swap_sems.at[3], cross)
     tokens_move = remote(swap_buf, moved, swap_sems.at[4], swap_sems.at[5], cross)
-    final_load = pltpu.make_async_copy(final_ref, final_buf, local_sems.at[4])
-    final_store = pltpu.make_async_copy(final_buf, output_ref, local_sems.at[5])
-
-    @pl.when(c != h)
-    def _():
-        output_move.start()
-
-    @pl.when(c == h)
-    def _():
-        final_load.start()
-
     width, low_width = hidden_ref.shape[1], latent_ref.shape[1]
     half = head_dim // 2
     dlatent, dgain_latent = norm_back_rows(dlow_ref[...], latent_ref[...], gain_latent_ref[...])
@@ -1785,20 +1793,13 @@
 
     @pl.when(c != h)
     def _():
-        output_move.wait()
         tokens_move.wait()
         tokens_ref[...] = moved[...].astype(wide)
 
-    @pl.when(c == h)
-    def _():
-        final_load.wait()
-        final_store.start()
-        final_store.wait()
-
 
 def shut(
     dlow, dkv, latent, gain_latent, cosine, sine, hidden, in_full, home, gain_one, dresid, dgain_two,
-    gate_terms, up_terms, head_terms, final, kept, across, part, order, number,
+    gate_terms, up_terms, head_terms, kept, across, part, order, number,
 ):
     count, width = hidden.shape
     head_dim = dkv.shape[1] // 2
@@ -1806,14 +1807,13 @@
     vmem, sem = pl.BlockSpec(memory_space=pltpu.VMEM), pltpu.SemaphoreType.DMA
     args = [
         dlow, dkv, latent, gain_latent, cosine, sine, hidden, in_full, home, gain_one, dresid,
-        dgain_two, gate_terms, up_terms, head_terms, final, kept, across,
+        dgain_two, gate_terms, up_terms, head_terms, kept, across,
     ]
-    hbm = {7, 12, 13, 14, 15, 17}
+    hbm = {7, 12, 13, 14, 16}
     ff = len(order) * len(order[0]) * part
     shapes = [
         ((rows, columns), wide),
         ((count, width), wide),
-        ((count, width), low),
         ((gate_terms.shape[1], ff), wide),
         ((up_terms.shape[1], ff), wide),
         ((head_terms.shape[1], 8 * head_terms.shape[2]), wide),
@@ -1823,7 +1823,7 @@
     return pl.pallas_call(
         functools.partial(shut_kernel, part, head_dim, order, len(args), len(shapes)),
         in_specs=[in_hbm() if i in hbm else vmem for i in range(len(args))],
-        out_specs=[in_hbm() if i == 2 else vmem for i in range(len(shapes))],
+        out_specs=[vmem] * len(shapes),
         out_shape=[jax.ShapeDtypeStruct(*s) for s in shapes],
         scratch_shapes=[
             pltpu.VMEM(in_full.shape, low),
@@ -1838,7 +1838,6 @@
             pltpu.VMEM(gate_terms.shape, low),
             pltpu.VMEM(up_terms.shape, low),
             pltpu.VMEM(head_terms.shape, low),
-            pltpu.VMEM((count, width), low),
             pltpu.VMEM(across.shape, low),
             sem((32,)),
             sem((32,)),
@@ -2216,12 +2215,10 @@
 
     scale_one = rms_scale(inputs)
     if natural:
-        packed, hidden, latent, cosine, sine, gate_a_h, gate_b_h = front(
+        packed, hidden, latent, cosine, sine, own_cos, own_sin, gate_a_h, gate_b_h = front(
             ends, home, in_full, gain_one[None], gain_latent[None], mapped_rates[None], row_len, 2,
             ("h", "h"), (gate_a, gate_b),
         )
-        own_cos = lax.dynamic_slice_in_dim(cosine, me * count, count)
-        own_sin = lax.dynamic_slice_in_dim(sine, me * count, count)
         packed, heads_x, up_a = together(packed, heads_x, up_a)
         up_a_h, up_b_h = flip(up_a, "h"), flip(after(up_b, packed), "h")
         gate_x = [flip(a, "x") for a in (gate_a, gate_b, gate_a_h, gate_b_h)]
@@ -2310,18 +2307,18 @@
     branch = dresid.astype(low)
     if natural:
         by_h = (2, 2, -1, ff_pad)
-        dlow, dkv, gate_terms, up_terms, final, out_terms, head_terms, *_ = middle(
+        dlow, dkv, gate_terms, up_terms, output, out_terms, head_terms, *_ = middle(
             ends, branch, (gate_terms.reshape(by_h), gate_x.reshape(by_h)),
             (up_terms.reshape(by_h), up_x.reshape(by_h)), spread, query, mixed, packed, logs, cosine,
             sine, out_own, up_query, resid, heads, scale, 7,
         )
         gate_terms, up_terms = [a.reshape(n_group, shard, ff_pad) for a in (gate_terms, up_terms)]
         head_terms = head_terms.reshape(n_group, rows_up, heads * head_dim)
-        summed, grad_tokens, output, grad_gate, grad_upward, grad_uquery, grad_out = shut(
+        summed, grad_tokens, grad_gate, grad_upward, grad_uquery, grad_out = shut(
             dlow, dkv, latent, gain_latent[None], own_cos, own_sin, hidden,
             in_full.reshape(n_dev, shard, -1), home, gain_one[None], dresid, dgain_two[None],
-            gate_terms, up_terms, head_terms, final, pick(out_terms, h), pick(out_terms, 1 - h),
-            ff_part, order, 9,
+            gate_terms, up_terms, head_terms, pick(out_terms, h), pick(out_terms, 1 - h), ff_part,
+            order, 9,
         )
     else:
         branch_all = gather_row(branch, 7)

time: 591 us -> 588 us (level)
    pallas_call x1, Pallas kernels: 77.7 us -> 67.8 us  [shut(): pl.pallas_call(functools.partial(shut_kernel, part, head_dim, order, len(...]
    pallas_call x1, Pallas kernels: 127 us -> 136 us  [middle(): pl.pallas_call(functools.partial(middle_kernel, heads, tile_of(length), s...]
    unnamed x105 -> x111, local copies, waits for them, and re-layouts: 27 us -> 26.7 us
  transfers between devices with their start and end apart: 11 -> 11, of which waited for: 2 -> 2; matrix products, arithmetic and copies ran while one was open for 1% -> 0% of each run, Pallas kernels for 19% -> 19%
where the time goes in v1:
time: 588 us; the launch traced here: 582 us
  Pallas kernels  516 us (88%)
  local copies, waits for them, and re-layouts  37.1 us (6%)
  starting transfers between devices  12.3 us (2%)
  waiting for transfers between devices  8.51 us (1%)
  other arithmetic  7.09 us (1%)
    pallas_call x1, Pallas kernels, middle(): pl.pallas_call(functools.partial(middle_kernel, heads, tile_of(length), s...  136 us
    pallas_call x1, Pallas kernels, feed_back(): pl.pallas_call(functools.partial(feed_back_kernel, True, chunks), in_spec...  67.9 us
    pallas_call x1, Pallas kernels, shut(): pl.pallas_call(functools.partial(shut_kernel, part, head_dim, order, len(...  67.8 us
    pallas_call x1, Pallas kernels, feed_forward(): pl.pallas_call(functools.partial(feed_kernel, False, chunks), in_specs=[i...  67.1 us
    pallas_call x1, Pallas kernels, open_exchange(): pl.pallas_call(functools.partial(open_kernel, n_swaps, part, order), in_s...  66.4 us
    pallas_call x1, Pallas kernels, front(): pl.pallas_call(functools.partial(front_kernel, kinds), in_specs=[pl.Block...  48.5 us
    pallas_call x1, Pallas kernels, scatter_row(): pl.pallas_call(functools.partial(scatter_kernel, even, chunks, n, kinds),...  39.8 us
    unnamed x111, local copies, waits for them, and re-layouts  26.7 us
  transfers between devices with their start and end apart: 11, of which 2 were waited for; matrix products, arithmetic and copies ran while one was open for 0% of the time, Pallas kernels for 19%

profile of v1, /device:TPU:0, one launch (start us, length us, event | category | flops | bytes accessed | tf_op | source)
XLA Modules:
  0.0 582.4 jit_solution(16075588890672382005)
XLA Ops:
  0.7 1.2 reshape.255
  2.0 0.2 copy.29
  2.2 0.2 reshape.256.heads_in
  2.4 0.2 scatter.11
  2.6 0.2 scatter.14
  2.8 1.1 copy-done.10
  4.0 1.1 copy-done.11
  5.1 1.1 copy-done.12
  6.2 66.4 %open_exchange.1 = (bf16[32,64,1664]{2,1,0:T(8,128)(2,1)S(1)}, bf16[2,128,2048]{2,1,0:T(8,128)(2,1)}, bf16[2,2,2,4,32,512]{5,4,3,2,1,0:T(8,128)(2,1)S(1)}, bf16[...) custom-call(bf16[64,1664]{1,0:T(8,128)(2,1)S(1)} %pad_maximum_fusion, ...), custom_call_target="tpu_custom_call" | custom-call | bytes 157286400 | tf_op jit(solution)/shard_map/open_exchange/pallas_call | solution.py:360
  72.6 1.0 copy-done.20
  73.6 1.0 collective-permute-start
  74.7 1.1 collective-permute-start.3
  75.7 0.8 copy-done
  76.6 0.1 convert_reduce_fusion
  76.7 0.1 reshape.271.gain_ref.refs_9_
  76.8 0.9 convert_reduce_fusion.1
  77.7 0.1 reshape.272.low_gain_ref.refs_3_
  77.7 0.2 reduce-window.9
  77.9 2.9 copy-done.1
  80.9 48.5 %front.1 = (bf16[8,192,1536]{2,1,0:T(8,128)(2,1)S(1)}, bf16[192,2048]{1,0:T(8,128)(2,1)S(1)}, f32[192,1024]{1,0:T(8,128)S(1)}, f32[1536,128]{1,0:T(8,128)S(1)}, ...) custom-call(s32[8]{0:T(128)S(1)} %bitcast.46, ...), custom_call_target="tpu_custom_call" | custom-call | bytes 104857600 | tf_op jit(solution)/shard_map/front/pallas_call | solution.py:472
  129.4 0.9 copy-done.8
  130.3 2.1 copy-done.19
  132.5 0.9 copy-done.21
  133.3 0.9 copy-done.22
  134.3 2.0 collective-permute-start.6
  136.4 0.1 collective-permute-start.2
  136.5 2.9 collective-permute-start.1
  139.4 22.5 %attend.1 = (bf16[1536,512]{1,0:T(8,128)(2,1)}, bf16[1536,512]{1,0:T(8,128)(2,1)}, f32[2,1536,128]{2,1,0:T(8,128)}, bf16[1536,2048]{1,0:T(8,128)(2,1)}, bf16[512,2048]{1,0:T(8,128)(2,1)}) custom-call(s32[8]{0:T(128)} %bitcast.47, bf16[1536,1536]{1,0:T(8,128)(2,1)} %bitcast.49, bf16[1024,512]{1,0:T(8,128)(2,1)} %bitcast.51, f32[1536,128]{1,0:T(8,128)} %copy-done.21, ...), custom_call_target="tpu_custom_call" | custom-call | flops 14495514624 | bytes 12582912 | tf_op jit(solution)/shard_map/attend/pallas_call | solution.py:2025
  161.9 1.1 collective-permute-done.2.refs_12_.refs_16_
  163.0 0.9 collective-permute-start.4
  163.9 7.4 %collective-permute-done.1.refs_11_.refs_15_ = bf16[256,768]{1,0:T(8,128)(2,1)} collective-permute-done((bf16[256,768]{1,0:T(8,128)(2,1)S(1)}, bf16[256,768]{1,0:T(8,128)(2,1)}, u32[]{:S(2)}, u32[]{:S(2)}) %collective-permute-start.1) | collective-permute-done | bytes 393248 | tf_op jit(solution)/shard_map/ppermute | solution.py:72
  171.3 0.9 collective-permute-start.8
  172.3 1.2 collective-permute-start.7
  173.5 0.9 collective-permute-start.10
  174.4 1.2 collective-permute-start.9
  175.7 3.0 copy-done.3
  178.8 39.8 %scatter_row.1 = (f32[192,2048]{1,0:T(8,128)S(1)}, bf16[176,1024]{1,0:T(8,128)(2,1)S(1)}, bf16[176,1024]{1,0:T(8,128)(2,1)S(1)}) custom-call(bf16[8,192,2048]{2,1,0:T(8,128)(2,1)S(1)} %bitcast.37, bf16[176,1024]{1,0:T(8,128)(2,1)S(1)} %get-tuple-element.206.refs_1_.refs_17_.refs_21_, bf16[176,1024]{1,0:T(8,128)(2,1)S(1)} %get-tuple-element.205.refs_2_.refs_19_.refs_25_), custom_call_target="tpu_custom_call" | custom-call | bytes 83886080 | tf_op jit(solution)/shard_map/scatter_row/pallas_call | solution.py:1191
  218.7 0.3 multiply_reduce_fusion.2
  219.0 0.4 copy-done.25
  219.4 0.1 copy-done.26
  219.5 0.1 copy-done.51
  219.6 1.1 copy-done.27
  220.8 1.1 multiply_convert_fusion.refs_0_
  221.8 67.1 %feed_forward.1 = (bf16[8,192,2048]{2,1,0:T(8,128)(2,1)}, bf16[8,192,768]{2,1,0:T(8,128)(2,1)}, bf16[8,192,768]{2,1,0:T(8,128)(2,1)}, bf16[8,192,768]{2,1,0:T(8,...) custom-call(bf16[192,2048]{1,0:T(8,128)(2,1)} %multiply_convert_fusi, ...), custom_call_target="tpu_custom_call" | custom-call | flops 9663676416 | bytes 104857600 | tf_op jit(solution)/shard_map/feed_forward/pallas_call | solution.py:805
  289.0 67.9 %feed_back.1 = (f32[192,2048]{1,0:T(8,128)}, bf16[4,192,2048]{2,1,0:T(8,128)(2,1)}, bf16[4,192,2048]{2,1,0:T(8,128)(2,1)}, bf16[1024,768]{1,0:T(8,128)(2,1)}, bf...) custom-call(bf16[8,192,2048]{2,1,0:T(8,128)(2,1)} %get-tuple-element, ...), custom_call_target="tpu_custom_call" | custom-call | flops 28991029248 | bytes 104857600 | tf_op jit(solution)/shard_map/feed_back/pallas_call | solution.py:1055
  357.0 2.6 multiply_reduce_fusion
  359.5 1.9 fusion
  361.5 135.8 %middle.1 = (f32[192,1024]{1,0:T(8,128)}, f32[192,512]{1,0:T(8,128)}, bf16[2,256,768]{2,1,0:T(8,128)(2,1)}, bf16[2,256,768]{2,1,0:T(8,128)(2,1)}, bf16[192,2048]...) custom-call(s32[8]{0:T(128)} %bitcast.48, ...), custom_call_target="tpu_custom_call" | custom-call | flops 21743271936 | bytes 209715200 | tf_op jit(solution)/shard_map/middle/pallas_call | solution.py:1573
  497.3 2.3 dynamic-slice_bitcast_fusion
  499.6 67.8 %shut.1 = (f32[64,1664]{1,0:T(8,128)}, f32[192,2048]{1,0:T(8,128)}, f32[64,5632]{1,0:T(8,128)}, f32[64,5632]{1,0:T(8,128)}, f32[32,4096]{1,0:T(8,128)}, /*index=5*/f32[128,2048]{1,0:T(8,128)}) custom-call(f32[192,1024]{1,0:T(8,128)} %get-tuple-element.174.refs_0_, f32[192,512]{1,0:T(8,128)} %get-tuple-element.175.refs_1_, f32[192,1024]{1,0:T(8,128)} %copy-done.9, ...), custom_call_target="tpu_custom_call" | custom-call | bytes 157286400 | tf_op jit(solution)/shard_map/shut/pallas_call | solution.py:1823
  567.4 1.8 slice.117
  569.2 1.5 fusion.4
  570.7 1.3 slice_bitcast_fusion
  572.0 1.2 slice_bitcast_fusion.1
  573.2 0.9 copy.39
  574.1 1.1 copy.40
  575.2 0.2 copy-done.38
  575.5 0.8 copy.41
  576.2 1.0 copy.42
  577.2 1.1 copy.43
  578.3 0.8 copy-done.32
  579.1 1.1 copy.44
  580.2 0.8 copy-done.31
  581.0 1.1 copy.45
  (107 shorter events, 0.5 us)
Async XLA Ops:
  0.6 1.7 copy-start.44
  0.7 1.7 copy-start.45
  0.7 1.7 copy-start.46
  0.7 1.9 copy-start.47
  0.7 2.1 copy-start.41
  0.7 2.1 copy-start.43
  0.7 2.1 copy-start.42
  0.7 2.1 copy-start.13
  2.8 1.1 copy-start.10
  4.0 1.1 copy-start.11
  5.1 1.1 copy-start.12
  72.6 1.0 copy-start.20
  73.5 3.0 copy-start
  73.5 145.2 %copy-start.2 = (bf16[192,2048]{1,0:T(8,128)(2,1)}, bf16[192,2048]{1,0:T(8,128)(2,1)S(1)}, u32[]{:S(2)}) copy-start(bf16[192,2048]{1,0:T(8,128)(2,1)S(1)} %get-tuple-element.121.home_ref.refs_8_) | copy-start | bytes 2359300
  73.6 62.9 %collective-permute-start = (bf16[256,2048]{1,0:T(8,128)(2,1)}, bf16[256,2048]{1,0:T(8,128)(2,1)}, u32[]{:S(2)}, u32[]{:S(2)}) collective-permute-start(bf16[256,2048]{1,0:T(8,128)(2,1)} %bitcast.10.own_ref), channel_id=1, source_target_pairs={{0,16},{16,0},{1,17},{17,1},{2,18},{18,2},{3,19},{19,3},{4,20},{20... | collective-permute-start | bytes 3145736 | tf_op jit(solution)/shard_map/ppermute | solution.py:72
  74.6 54.7 %copy-start.5 = (bf16[4,64,768]{2,1,0:T(8,128)(2,1)}, bf16[4,64,768]{2,1,0:T(8,128)(2,1)S(1)}, u32[]{:S(2)}) copy-start(bf16[4,64,768]{2,1,0:T(8,128)(2,1)S(1)} %get-tuple-element.204) | copy-start | bytes 1179652
  74.7 88.4 %copy-start.4 = (bf16[4,64,768]{2,1,0:T(8,128)(2,1)}, bf16[4,64,768]{2,1,0:T(8,128)(2,1)S(1)}, u32[]{:S(2)}) copy-start(bf16[4,64,768]{2,1,0:T(8,128)(2,1)S(1)} %get-tuple-element.203) | copy-start | bytes 1179652
  74.7 99.7 %collective-permute-start.3 = (bf16[256,768]{1,0:T(8,128)(2,1)S(1)}, bf16[256,768]{1,0:T(8,128)(2,1)S(1)}, u32[]{:S(2)}, u32[]{:S(2)}) collective-permute-start(bf16[256,768]{1,0:T(8,128)(2,1)S(1)} %bitcast.42), channel_id=1, source_target_pairs={{0,16},{16,0},{1,17},{17,1},{2,18},{18,2},{3,19},{19,3},{4,20},{20... | collective-permute-start | bytes 1179656 | tf_op jit(solution)/shard_map/ppermute | solution.py:72
  76.7 52.6 %copy-start.16 = (f32[1,2048]{1,0:T(1,128)}, f32[1,2048]{1,0:T(1,128)S(1)}, u32[]{:S(2)}) copy-start(f32[1,2048]{1,0:T(1,128)S(1)} %reshape.271.gain_ref.refs_9_) | copy-start | bytes 24580
  77.7 51.7 %copy-start.17 = (f32[1,1024]{1,0:T(1,128)}, f32[1,1024]{1,0:T(1,128)S(1)}, u32[]{:S(2)}) copy-start(f32[1,1024]{1,0:T(1,128)S(1)} %reshape.272.low_gain_ref.refs_3_) | copy-start | bytes 12292
  77.9 51.5 %copy-start.18 = (s32[8,1]{0,1:T(1,128)}, s32[8,1]{0,1:T(1,128)S(1)}, u32[]{:S(2)}) copy-start(s32[8,1]{0,1:T(1,128)S(1)} %reduce-window.9) | copy-start | bytes 100
  77.9 2.9 copy-start.1
  129.4 0.9 copy-start.8
  130.3 2.1 copy-start.19
  132.5 0.9 copy-start.21
  133.3 0.9 copy-start.22
  134.2 2.2 copy-start.14
  134.2 2.2 copy-start.15
  134.2 27.7 %copy-start.9 = (f32[192,1024]{1,0:T(8,128)}, f32[192,1024]{1,0:T(8,128)S(1)}, u32[]{:S(2)}) copy-start(f32[192,1024]{1,0:T(8,128)S(1)} %get-tuple-element.176.refs_2_) | copy-start | bytes 2359300
  134.2 27.7 %copy-start.23 = (bf16[256,768]{1,0:T(8,128)(2,1)}, bf16[256,768]{1,0:T(8,128)(2,1)S(1)}, u32[]{:S(2)}) copy-start(bf16[256,768]{1,0:T(8,128)(2,1)S(1)} %get-tuple-element.137.refs_3_.refs_7_) | copy-start | bytes 1179652
  134.2 27.7 %copy-start.24 = (bf16[256,768]{1,0:T(8,128)(2,1)}, bf16[256,768]{1,0:T(8,128)(2,1)S(1)}, u32[]{:S(2)}) copy-start(bf16[256,768]{1,0:T(8,128)(2,1)S(1)} %get-tuple-element.138.refs_4_.refs_8_) | copy-start | bytes 1179652
  134.2 38.0 %collective-permute-start.5 = (bf16[256,768]{1,0:T(8,128)(2,1)S(1)}, bf16[256,768]{1,0:T(8,128)(2,1)S(1)}, u32[]{:S(2)}, u32[]{:S(2)}) collective-permute-start(bf16[256,768]{1,0:T(8,128)(2,1)S(1)} %get-tuple-element.137.refs_3_.refs_7_), channel_id=1, source_target_pairs={{0,16},{16,0},{1,17},{17,1},{2,18},{18,2},{3,19},{19,3},{4,20},{20... | collective-permute-start | bytes 1179656 | tf_op jit(solution)/shard_map/ppermute | solution.py:72
  134.3 39.1 %collective-permute-start.6 = (bf16[256,768]{1,0:T(8,128)(2,1)S(1)}, bf16[256,768]{1,0:T(8,128)(2,1)S(1)}, u32[]{:S(2)}, u32[]{:S(2)}) collective-permute-start(bf16[256,768]{1,0:T(8,128)(2,1)S(1)} %get-tuple-element.138.refs_4_.refs_8_), channel_id=1, source_target_pairs={{0,16},{16,0},{1,17},{17,1},{2,18},{18,2},{3,19},{19,3},{4,20},{20... | collective-permute-start | bytes 1179656 | tf_op jit(solution)/shard_map/ppermute | solution.py:72
  136.4 34.9 %copy-start.39 = (bf16[4,64,768]{2,1,0:T(8,128)(2,1)}, bf16[4,64,768]{2,1,0:T(8,128)(2,1)S(1)}, u32[]{:S(2)}) copy-start(bf16[4,64,768]{2,1,0:T(8,128)(2,1)S(1)} %get-tuple-element.201) | copy-start | bytes 1179652
  136.4 35.8 %copy-start.40 = (bf16[4,64,768]{2,1,0:T(8,128)(2,1)}, bf16[4,64,768]{2,1,0:T(8,128)(2,1)S(1)}, u32[]{:S(2)}) copy-start(bf16[4,64,768]{2,1,0:T(8,128)(2,1)S(1)} %get-tuple-element.202) | copy-start | bytes 1179652
  136.4 26.6 %collective-permute-start.2 = (bf16[256,768]{1,0:T(8,128)(2,1)S(1)}, bf16[256,768]{1,0:T(8,128)(2,1)}, u32[]{:S(2)}, u32[]{:S(2)}) collective-permute-start(bf16[256,768]{1,0:T(8,128)(2,1)S(1)} %bitcast.56), channel_id=1, source_target_pairs={{0,4},{4,0},{1,5},{5,1},{2,6},{6,2},{3,7},{7,3},{8,12},{12,8},{9,1... | collective-permute-start | bytes 1179656 | tf_op jit(solution)/shard_map/ppermute | solution.py:72
  136.5 34.8 %collective-permute-start.1 = (bf16[256,768]{1,0:T(8,128)(2,1)S(1)}, bf16[256,768]{1,0:T(8,128)(2,1)}, u32[]{:S(2)}, u32[]{:S(2)}) collective-permute-start(bf16[256,768]{1,0:T(8,128)(2,1)S(1)} %bitcast.60), channel_id=1, source_target_pairs={{0,4},{4,0},{1,5},{5,1},{2,6},{6,2},{3,7},{7,3},{8,12},{12,8},{9,1... | collective-permute-start | bytes 1179656 | tf_op jit(solution)/shard_map/ppermute | solution.py:72
  139.4 36.2 %copy-start.37 = (bf16[176,2048]{1,0:T(8,128)(2,1)S(1)}, bf16[176,2048]{1,0:T(8,128)(2,1)}, u32[]{:S(2)}) copy-start(bf16[176,2048]{1,0:T(8,128)(2,1)} %param.33) | copy-start | bytes 2162692
  163.0 55.6 %collective-permute-start.4 = (bf16[256,768]{1,0:T(8,128)(2,1)S(1)}, bf16[256,768]{1,0:T(8,128)(2,1)}, u32[]{:S(2)}, u32[]{:S(2)}) collective-permute-start(bf16[256,768]{1,0:T(8,128)(2,1)S(1)} %bitcast.39), channel_id=1, source_target_pairs={{0,16},{16,0},{1,17},{17,1},{2,18},{18,2},{3,19},{19,3},{4,20},{20... | collective-permute-start | bytes 1179656 | tf_op jit(solution)/shard_map/ppermute | solution.py:72
  171.3 47.3 %collective-permute-start.8 = (bf16[256,768]{1,0:T(8,128)(2,1)S(1)}, bf16[256,768]{1,0:T(8,128)(2,1)}, u32[]{:S(2)}, u32[]{:S(2)}) collective-permute-start(bf16[256,768]{1,0:T(8,128)(2,1)S(1)} %bitcast.57), channel_id=1, source_target_pairs={{0,16},{16,0},{1,17},{17,1},{2,18},{18,2},{3,19},{19,3},{4,20},{20... | collective-permute-start | bytes 1179656 | tf_op jit(solution)/shard_map/ppermute | solution.py:72
  172.3 2.1 copy-start.49
  172.3 46.4 %collective-permute-start.7 = (bf16[256,768]{1,0:T(8,128)(2,1)S(1)}, bf16[256,768]{1,0:T(8,128)(2,1)}, u32[]{:S(2)}, u32[]{:S(2)}) collective-permute-start(bf16[256,768]{1,0:T(8,128)(2,1)S(1)} %bitcast.61), channel_id=1, source_target_pairs={{0,16},{16,0},{1,17},{17,1},{2,18},{18,2},{3,19},{19,3},{4,20},{20... | collective-permute-start | bytes 1179656 | tf_op jit(solution)/shard_map/ppermute | solution.py:72
  173.5 2.1 copy-start.50
  173.5 45.2 %collective-permute-start.10 = (bf16[256,768]{1,0:T(8,128)(2,1)}, bf16[256,768]{1,0:T(8,128)(2,1)}, u32[]{:S(2)}, u32[]{:S(2)}) collective-permute-start(bf16[256,768]{1,0:T(8,128)(2,1)} %collective-permute-done.2.refs_12_.refs_16_), channel_id=1, source_target_pairs={{0,16},{16,0},{1,17},{17,1},{2,18},{18,2},{3,19},{19,3},{4,20},{20... | collective-permute-start | bytes 1179656 | tf_op jit(solution)/shard_map/ppermute | solution.py:72
  174.4 44.2 %copy-start.48 = (bf16[256,768]{1,0:T(8,128)(2,1)}, bf16[256,768]{1,0:T(8,128)(2,1)S(1)}, u32[]{:S(2)}) copy-start(bf16[256,768]{1,0:T(8,128)(2,1)S(1)} %collective-permute-done.3.refs_5_.refs_9_) | copy-start | bytes 1179652
  174.4 44.3 %collective-permute-start.9 = (bf16[256,768]{1,0:T(8,128)(2,1)}, bf16[256,768]{1,0:T(8,128)(2,1)S(1)}, u32[]{:S(2)}, u32[]{:S(2)}) collective-permute-start(bf16[256,768]{1,0:T(8,128)(2,1)} %collective-permute-done.1.refs_11_.refs_15_), channel_id=1, source_target_pairs={{0,16},{16,0},{1,17},{17,1},{2,18},{18,2},{3,19},{19,3},{4,20},{20... | collective-permute-start | bytes 1179656 | tf_op jit(solution)/shard_map/ppermute | solution.py:72
  175.7 42.9 %copy-start.6 = (bf16[176,1024]{1,0:T(8,128)(2,1)}, bf16[176,1024]{1,0:T(8,128)(2,1)S(1)}, u32[]{:S(2)}) copy-start(bf16[176,1024]{1,0:T(8,128)(2,1)S(1)} %get-tuple-element.205.refs_2_.refs_19_.refs_25_) | copy-start | bytes 1081348
  175.7 42.9 %copy-start.7 = (bf16[176,1024]{1,0:T(8,128)(2,1)}, bf16[176,1024]{1,0:T(8,128)(2,1)S(1)}, u32[]{:S(2)}) copy-start(bf16[176,1024]{1,0:T(8,128)(2,1)S(1)} %get-tuple-element.206.refs_1_.refs_17_.refs_21_) | copy-start | bytes 1081348
  175.7 3.0 copy-start.3
  218.6 0.8 copy-start.25
  218.6 0.9 copy-start.26
  218.7 0.9 copy-start.51
  219.6 1.1 copy-start.27
  289.0 68.0 %copy-start.28 = (f32[192,2048]{1,0:T(8,128)S(1)}, f32[192,2048]{1,0:T(8,128)}, u32[]{:S(2)}) copy-start(f32[192,2048]{1,0:T(8,128)} %copy-done.27) | copy-start | bytes 4718596
  357.0 2.6 copy-start.29
  357.0 2.6 copy-start.35
  499.6 73.6 %copy-start.36 = (bf16[192,2048]{1,0:T(8,128)(2,1)S(1)}, bf16[192,2048]{1,0:T(8,128)(2,1)}, u32[]{:S(2)}) copy-start(bf16[192,2048]{1,0:T(8,128)(2,1)} %get-tuple-element.226) | copy-start | bytes 2359300
  567.4 6.7 %copy-start.30 = (f32[192,2048]{1,0:T(8,128)S(1)}, f32[192,2048]{1,0:T(8,128)}, u32[]{:S(2)}) copy-start(f32[192,2048]{1,0:T(8,128)} %get-tuple-element.227) | copy-start | bytes 4718596
  574.1 1.4 copy-start.38
  574.1 2.2 copy-start.34
  575.4 1.8 copy-start.33
  577.2 1.9 copy-start.32
  579.1 1.9 copy-start.31
